TPU v7x, 32 devices: a whole 2x2x4 slice. The times are simulated.
32 devices in a mesh: gx: 2 (over x), gy: 16 (over z, y, core).
Axes of the slice: x: 2, y: 2, z: 4, core: 2. Of those that a mesh axis runs over, the one named last changes fastest.
Arguments:
- level_set: float32 [16, 512, 128], P('gx', 'gy'), may hold values from -3 to 3
- velocity: float32 [3, 16, 512, 128], P(None, 'gx', 'gy'), may hold values from -5 to 5
- source: float32 [16, 512, 128], P('gx', 'gy'), may hold values from -6 to 6
- wick_solid: int32 [2, 64, 16], P('gx', 'gy'), may hold values 0 or 1
Outputs:
- level_new: float32 [16, 512, 128], P('gx', 'gy')
- pressure: float32 [16, 512, 128], P('gx', 'gy')
All inputs are finite; a program needn't handle non-finite values. No bound on the sum of `wick_solid` on one device may be relied on, other than what follows from the above.
Results may differ from a plain program's by a relative error of at most 0.00055.
Values sent between devices are 32-bit elements; how exact they have to be, the bound alone decides.
A program may use at most 64 MiB of HBM per device.

v0:
```python
import functools

import jax
import jax.numpy as jnp
import ml_dtypes
import numpy as np
from jax import lax
from jax.experimental import pallas as pl
from jax.experimental.pallas import tpu as pltpu
from jax.sharding import PartitionSpec as P

EZ = 1
EY = 4
EX = 16
ROWS = 256
EXT = 384
SPEC = 400

TIME_STEP = 0.02
HELM_COEF = 0.25
LEVEL_WIDTH = 0.25
GAS_RATIO = 10.0
SOLID_FACTOR = 0.25
SCHWARZ_SCALE = 0.5
SCHWARZ_SHIFT = 0.05

MESH = pl.DeviceIdType.MESH
F32 = jnp.float32
BF16 = jnp.bfloat16

SIDES = ((-1, 0), (1, 0), (0, -1), (0, 1), (-1, -1), (-1, 1), (1, -1), (1, 1))
OPPOSITE = tuple(SIDES.index((-dz, -dy)) for dz, dy in SIDES)


def gll_tables():
    nodes = np.array(
        [
            -1.0,
            -0.8717401485096066,
            -0.5917001814331423,
            -0.2092992179024789,
            0.2092992179024789,
            0.5917001814331423,
            0.8717401485096066,
            1.0,
        ]
    )
    weight = np.array(
        [
            1.0 / 28.0,
            0.21070422714350603,
            0.3411226924835044,
            0.4124587946587038,
            0.4124587946587038,
            0.3411226924835044,
            0.21070422714350603,
            1.0 / 28.0,
        ]
    )
    bary = np.array(
        [1.0 / np.prod([nodes[i] - nodes[j] for j in range(8) if j != i]) for i in range(8)]
    )
    deriv = np.zeros((8, 8))
    for i in range(8):
        for j in range(8):
            if i != j:
                deriv[i, j] = bary[j] / bary[i] / (nodes[i] - nodes[j])
        deriv[i, i] = -np.sum(deriv[i])
    return weight, deriv


def halves(table):
    table = np.asarray(table, np.float32)
    high = table.astype(ml_dtypes.bfloat16)
    low = (table - high.astype(np.float32)).astype(ml_dtypes.bfloat16)
    return high, low


def tables():
    weight, deriv = gll_tables()
    ids = np.arange(10) + 1.0
    sine = np.sqrt(2.0 / 11.0) * np.sin(np.pi * np.outer(ids, ids) / 11.0)
    eig = 2.0 - 2.0 * np.cos(np.pi * ids / 11.0)
    dz = np.kron(deriv, np.eye(32))
    dy = np.kron(np.eye(32), deriv)
    grad = np.concatenate([dz, dy], axis=0)
    dx_t = np.kron(np.eye(EX), deriv.T)
    dx = np.kron(np.eye(EX), deriv)

    def ext_row(z, y):
        zlo, zhi, ylo, yhi = z < 0, z > 7, y < 0, y > 31
        if zlo or zhi:
            if ylo or yhi:
                return 336 + 2 * int(zhi) + int(yhi)
            return 256 + 32 * int(zhi) + y
        if ylo or yhi:
            return 320 + 8 * int(yhi) + z
        return 32 * z + y

    widen = np.zeros((SPEC, EXT))
    for zi in range(10):
        z = zi - 1
        for e in range(EY):
            for yi in range(10):
                y = 8 * e - 2 if yi == 0 else (8 * e + 9 if yi == 9 else 8 * e + yi - 1)
                widen[zi * 40 + e * 10 + yi, ext_row(z, y)] = 1.0
    spec_zy = np.kron(sine, np.kron(np.eye(EY), sine)) @ widen
    widen_x = np.zeros((160, 128))
    for e in range(EX):
        for xi in range(10):
            x = 8 * e - 2 if xi == 0 else (8 * e + 9 if xi == 9 else 8 * e + xi - 1)
            if 0 <= x < 128:
                widen_x[e * 10 + xi, x] = 1.0
    spec_x = np.zeros((128, 256))
    spec_x[:, :160] = (np.kron(np.eye(EX), sine) @ widen_x).T
    back_zy = np.kron(sine[1:9], np.kron(np.eye(EY), sine[1:9]))
    back_x = np.zeros((256, 128))
    back_x[:160] = np.kron(np.eye(EX), sine[1:9]).T
    lam_zy = (eig[:, None] + np.tile(eig, EY)[None, :]).reshape(SPEC)
    inv_den = np.zeros((SPEC, 256))
    inv_den[:, :160] = 1.0 / (
        SCHWARZ_SCALE * (lam_zy[:, None] + np.tile(eig, EX)[None, :]) + SCHWARZ_SHIFT
    )
    mass = 0.125 * (
        np.kron(weight, np.tile(weight, EY))[:, None] * np.tile(weight, EX)[None, :]
    )
    out = []
    for table in (grad, grad.T, dx_t, dx, spec_zy, spec_x, back_zy, back_x):
        out.extend(halves(table))
    spread = np.kron(np.eye(EX), np.ones((1, 8)))
    out += [inv_den.astype(np.float32), mass.astype(np.float32), spread.astype(np.float32)]
    return out


def split(v):
    high = v.astype(BF16)
    low = (v - high.astype(F32)).astype(BF16)
    return high, low


def dot(a, b):
    return jnp.dot(a, b, preferred_element_type=F32)


def left(high_ref, low_ref, v, rows=None):
    pick = slice(None) if rows is None else rows
    vh, vl = split(v)
    both = dot(high_ref[pick, :], jnp.concatenate([vh, vl], axis=1))
    return both[:, :128] + both[:, 128:] + dot(low_ref[pick, :], vh)


def right(v, high_ref, low_ref):
    vh, vl = split(v)
    return dot(vh, high_ref[...]) + dot(vl, high_ref[...]) + dot(vh, low_ref[...])


def total(v):
    return jnp.sum(jnp.sum(v, axis=0, keepdims=True), axis=1, keepdims=True)


def sweep_step(a, row, col, k, sub, lane):
    pivot = jnp.sum(jnp.where(lane[:1] == k, row, 0.0), axis=1, keepdims=True)
    row_m = jnp.where(lane[:1] == k, -1.0, row) / pivot
    col_m = jnp.where(sub == k, -1.0, col)
    return jnp.where(jnp.logical_or(lane == k, sub == k), 0.0, a) - col_m * row_m


def kernel(
    ngx, ngy,
    level_ref, vel_ref, source_ref, solid_ref,
    gh, gl, gth, gtl, dxth, dxtl, dxh, dxl, szh, szl, sxh, sxl, bzh, bzl, bxh, bxl,
    inv_den_ref, mass_ref, spread_ref,
    level_out, pressure_out,
    flux_ref, invm_ref, part_ref, lev_ref, app_ref, res_ref, search_ref, a_ref,
    zs, zr, ys, yr, cs, cr, gbuf,
    send_sem, recv_sem, gsend_sem, grecv_sem,
):
    n = ngx * ngy
    ix = lax.axis_index("gx")
    iy = lax.axis_index("gy")
    me = ix * ngy + iy

    zr[...] = jnp.zeros_like(zr)
    yr[...] = jnp.zeros_like(yr)
    cr[...] = jnp.zeros_like(cr)

    barrier = pltpu.get_barrier_semaphore()

    def greet(i, carry):
        dst = lax.rem(me + i, n)
        pl.semaphore_signal(
            barrier, inc=1, device_id=(dst // ngy, lax.rem(dst, ngy)), device_id_type=MESH
        )
        return carry

    lax.fori_loop(1, n, greet, 0)

    has_zlo, has_zhi = ix > 0, ix < ngx - 1
    has_ylo, has_yhi = iy > 0, iy < ngy - 1

    def exists(d):
        dz, dy = SIDES[d]
        conds = []
        if dz:
            conds.append(has_zlo if dz < 0 else has_zhi)
        if dy:
            conds.append(has_ylo if dy < 0 else has_yhi)
        return conds[0] if len(conds) == 1 else jnp.logical_and(*conds)

    def buffers(r, d, layers):
        if d < 2:
            return zs.at[r, d, pl.ds(0, 32 * layers)], zr.at[r, OPPOSITE[d], pl.ds(0, 32 * layers)]
        if d < 4:
            return (
                ys.at[r, d - 2, pl.ds(0, 8 * layers)],
                yr.at[r, OPPOSITE[d] - 2, pl.ds(0, 8 * layers)],
            )
        return cs.at[r, d - 4], cr.at[r, OPPOSITE[d] - 4]

    def halo_copy(r, d, layers):
        src, dst = buffers(r, d, layers)
        dz, dy = SIDES[d]
        return pltpu.make_async_remote_copy(
            src_ref=src,
            dst_ref=dst,
            send_sem=send_sem.at[r, d],
            recv_sem=recv_sem.at[r, OPPOSITE[d]],
            device_id=(ix + dz, iy + dy),
            device_id_type=MESH,
        )

    def halo_send(r, layers, second=None):
        for s in range(2):
            zo, zi = ((0, 32), (224, 192))[s]
            zs[r, s, 0:32] = part_ref[zo : zo + 32]
            yo, yi = ((0, 1), (31, 30))[s]
            ys[r, s, 0:8] = part_ref[pl.ds(yo, 8, stride=32), :]
            if layers > 1:
                zs[r, s, 32:64] = part_ref[zi : zi + 32]
                ys[r, s, 8:16] = part_ref[pl.ds(yi, 8, stride=32), :]
            if second is not None:
                zs[r, s, 64:96] = second[zo : zo + 32]
                ys[r, s, 16:24] = second[pl.ds(yo, 8, stride=32), :]
        for c in range(4):
            dz, dy = SIDES[4 + c]
            zo, zi = (0, 32) if dz < 0 else (224, 192)
            yo, yi = (0, 1) if dy < 0 else (31, 30)
            cs[r, c, 0:1] = part_ref[zo + yo : zo + yo + 1]
            if layers > 1:
                cs[r, c, 1:2] = part_ref[zo + yi : zo + yi + 1]
                cs[r, c, 2:3] = part_ref[zi + yo : zi + yo + 1]
                cs[r, c, 3:4] = part_ref[zi + yi : zi + yi + 1]
            if second is not None:
                cs[r, c, 4:5] = second[zo + yo : zo + yo + 1]
        for d in range(8):

            @pl.when(exists(d))
            def _():
                halo_copy(r, d, layers).start()

    def halo_wait(r, layers):
        for d in range(8):

            @pl.when(exists(d))
            def _():
                src, _ = buffers(r, d, layers)
                _, dst = buffers(r, OPPOSITE[d], layers)
                dz, dy = SIDES[d]
                pltpu.make_async_remote_copy(
                    src_ref=src,
                    dst_ref=dst,
                    send_sem=send_sem.at[r, d],
                    recv_sem=recv_sem.at[r, d],
                    device_id=(ix + dz, iy + dy),
                    device_id_type=MESH,
                ).wait_recv()

    def halo_drain(r, layers):
        for d in range(8):

            @pl.when(exists(d))
            def _():
                halo_copy(r, d, layers).wait_send()

    def add_rim(r, ref, zoff, yoff, crow):
        ref[0:32] = ref[0:32] + zr[r, 0, zoff : zoff + 32]
        ref[224:256] = ref[224:256] + zr[r, 1, zoff : zoff + 32]
        for s, yo in ((0, 0), (1, 31)):
            at = pl.ds(yo, 8, stride=32)
            ref[at, :] = ref[at, :] + yr[r, s, yoff : yoff + 8]
        for c, row in enumerate((0, 31, 224, 255)):
            ref[row : row + 1] = ref[row : row + 1] + cr[r, c, crow : crow + 1]

    def outer_halo(r, ref):
        for s in range(2):
            base = 256 + 32 * s
            ref[base : base + 32] = zr[r, s, 32:64]
            ref[base : base + 1] = ref[base : base + 1] + cr[r, 2 * s, 2:3]
            ref[base + 31 : base + 32] = ref[base + 31 : base + 32] + cr[r, 2 * s + 1, 2:3]
            base = 320 + 8 * s
            ref[base : base + 8] = yr[r, s, 8:16]
            ref[base : base + 1] = ref[base : base + 1] + cr[r, s, 1:2]
            ref[base + 7 : base + 8] = ref[base + 7 : base + 8] + cr[r, 2 + s, 1:2]
        ref[336:384] = jnp.zeros((48, 128), F32)
        for c in range(4):
            ref[336 + c : 337 + c] = cr[r, c, 3:4]

    def gather_copy(g, dst):
        return pltpu.make_async_remote_copy(
            src_ref=gbuf.at[g, me],
            dst_ref=gbuf.at[g, me],
            send_sem=gsend_sem.at[g],
            recv_sem=grecv_sem.at[g],
            device_id=(dst // ngy, lax.rem(dst, ngy)),
            device_id_type=MESH,
        )

    def gather_send(g, first, second=None):
        gbuf[g, me, 0:1] = jnp.broadcast_to(first, (1, 128))
        if second is not None:
            gbuf[g, me, 1:2] = jnp.broadcast_to(second, (1, 128))

        def send(i, carry):
            gather_copy(g, lax.rem(me + i, n)).start()
            return carry

        lax.fori_loop(1, n, send, 0)

    def gather_bytes(g, sem):
        ref = gbuf.at[g, pl.ds(0, n - 1)]
        pltpu.make_async_copy(ref, ref, sem).wait()

    def gather_wait(g):
        gather_bytes(g, grecv_sem.at[g])

    row = lax.broadcasted_iota(jnp.int32, (ROWS, 128), 0)
    lane = lax.broadcasted_iota(jnp.int32, (ROWS, 128), 1)
    zpos, ypos = row // 32, row % 32
    y8, x8 = row % 8, lane % 8
    y_first = jnp.logical_and(y8 == 0, ypos > 0).astype(F32)
    y_last = jnp.logical_and(y8 == 7, ypos < 31).astype(F32)
    x_first = jnp.logical_and(x8 == 0, lane > 0).astype(F32)
    x_last = jnp.logical_and(x8 == 7, lane < 127).astype(F32)

    def flag(c):
        return c.astype(jnp.int32).astype(F32)

    zlo_f, zhi_f, ylo_f, yhi_f = flag(has_zlo), flag(has_zhi), flag(has_ylo), flag(has_yhi)
    z0, z7 = (zpos == 0).astype(F32), (zpos == 7).astype(F32)
    yb0, yb31 = (ypos == 0).astype(F32), (ypos == 31).astype(F32)
    half_zlo, half_zhi = 0.5 * zlo_f * z0, 0.5 * zhi_f * z7
    half_ylo, half_yhi = 0.5 * ylo_f * yb0, 0.5 * yhi_f * yb31
    own_z, own_y = 1.0 - half_zlo - half_zhi, 1.0 - half_ylo - half_yhi
    inv_m = (
        own_z
        * (own_y - 0.5 * (y_first + y_last))
        * (1.0 - 0.5 * (x_first + x_last))
    )
    invm_ref[...] = inv_m

    def fold_in(v):
        v = v + x_first * pltpu.roll(v, 1, 1) + x_last * pltpu.roll(v, 127, 1)
        return v + y_first * pltpu.roll(v, 1, 0) + y_last * pltpu.roll(v, ROWS - 1, 0)

    mass = mass_ref[...]
    level = level_ref[...]
    grads = left(gh, gl, level)
    advect = (
        vel_ref[0:ROWS] * grads[:ROWS]
        + vel_ref[ROWS : 2 * ROWS] * grads[ROWS:]
        + vel_ref[2 * ROWS : 3 * ROWS] * right(level, dxth, dxtl)
    )
    lev_ref[...] = fold_in(mass * (level - (2.0 * TIME_STEP) * advect))
    diverge = (
        left(gh, gl, vel_ref[0:ROWS], slice(0, ROWS))
        + left(gh, gl, vel_ref[ROWS : 2 * ROWS], slice(ROWS, 2 * ROWS))
        + right(vel_ref[2 * ROWS : 3 * ROWS], dxth, dxtl)
    )
    part_ref[...] = fold_in(mass * (source_ref[...] - (2.0 * TIME_STEP) * diverge))

    pl.semaphore_wait(barrier, n - 1)
    halo_send(0, 3, lev_ref)
    res_ref[0:ROWS] = part_ref[...]
    solid = dot(solid_ref[0].astype(F32), spread_ref[...])
    solid = jnp.concatenate(
        [jnp.broadcast_to(solid[e : e + 1], (8, 128)) for e in range(EY)], axis=0
    )
    solid = jnp.concatenate([solid] * 8, axis=0)
    halo_wait(0, 3)
    add_rim(0, res_ref, 0, 0, 0)
    add_rim(0, lev_ref, 64, 16, 4)
    outer_halo(0, res_ref)
    level_new = lev_ref[...] * inv_m / mass
    level_out[...] = level_new
    coef = (GAS_RATIO - (GAS_RATIO - 1.0) * jax.nn.sigmoid(level_new / LEVEL_WIDTH)) * (
        1.0 - (1.0 - SOLID_FACTOR) * solid
    )
    flux_ref[...] = 4.0 * coef * mass
    gather_send(0, total(coef) / (ROWS * 128.0), total(res_ref[0:ROWS] * inv_m))

    def local_solve():
        spectral = right(left(szh, szl, res_ref[...]), sxh, sxl) * inv_den_ref[...]
        return left(bzh, bzl, right(spectral, bxh, bxl))

    def helm(v):
        grads = left(gh, gl, v)
        flux = flux_ref[...]
        out = left(gth, gtl, jnp.concatenate([flux * grads[:ROWS], flux * grads[ROWS:]], axis=0))
        out = out + right(flux * right(v, dxth, dxtl), dxh, dxl)
        return out + HELM_COEF * mass_ref[...] * v

    npad = a_ref.shape[1]
    sub_n = lax.broadcasted_iota(jnp.int32, (n, npad), 0)
    lane_n = lax.broadcasted_iota(jnp.int32, (n, npad), 1)

    def gathered(g, item):
        got = gbuf[g, :, item, :]
        return got if npad == 128 else jnp.concatenate([got] * (npad // 128), axis=1)

    def invert(k_col):
        diag = lane_n == sub_n
        k_row = jnp.sum(jnp.where(diag, k_col, 0.0), axis=0, keepdims=True)
        gap = lane_n - sub_n
        same = lane_n // ngy == sub_n // ngy
        y_link = jnp.logical_and(jnp.logical_or(gap == 1, gap == -1), same)
        z_link = jnp.logical_or(gap == ngy, gap == -ngy)
        rate = jnp.where(z_link, float(EY * EX) / EZ, 0.0) + jnp.where(
            y_link, float(EZ * EX) / EY, 0.0
        )
        rate = jnp.where(lane_n < n, rate, 0.0)
        link = 2.0 * k_col * k_row / (k_col + k_row) * rate
        diagonal = HELM_COEF * EZ * EY * EX + jnp.sum(link, axis=1, keepdims=True)
        a = jnp.where(diag, diagonal, -link)
        if n <= 64:
            for k in range(n):
                a = sweep_step(a, a[k : k + 1, :], a[:, k : k + 1], k, sub_n, lane_n)
            a_ref[...] = a
        else:
            a_ref[...] = a

            def step(k, carry):
                a = a_ref[...]
                row = a_ref[pl.ds(k, 1), :]
                col = jnp.sum(jnp.where(lane_n == k, a, 0.0), axis=1, keepdims=True)
                a_ref[...] = sweep_step(a, row, col, k, sub_n, lane_n)
                return carry

            lax.fori_loop(0, n, step, 0)

    def coarse(t_col):
        x = -jnp.sum(a_ref[...] * t_col, axis=0, keepdims=True)
        t_row = jnp.sum(jnp.where(lane_n == sub_n, t_col, 0.0), axis=0, keepdims=True)
        return x, jnp.sum(x * t_row, axis=1, keepdims=True)

    def coarse_field(x):
        def value(dz, dy):
            at = me + dz * ngy + dy
            return jnp.sum(jnp.where(lane_n[:1] == at, x, 0.0), axis=1, keepdims=True)

        def along_y(dz):
            return own_y * value(dz, 0) + half_ylo * value(dz, -1) + half_yhi * value(dz, 1)

        return own_z * along_y(0) + half_zlo * along_y(-1) + half_zhi * along_y(1)

    local = local_solve() * inv_m
    part_ref[...] = fold_in(local)
    halo_send(1, 1)
    rz_part = total(res_ref[0:ROWS] * local)
    gather_wait(0)
    invert(gathered(0, 0))
    x, rz_coarse = coarse(gathered(0, 1))
    field = coarse_field(x)
    halo_wait(1, 1)
    search_ref[...] = part_ref[...]
    add_rim(1, search_ref, 0, 0, 0)
    search = search_ref[...] + field
    search_ref[...] = search

    applied = helm(search)
    gather_send(1, rz_part, total(search * applied))
    part_ref[...] = fold_in(applied)
    halo_send(2, 2)
    app_ref[0:ROWS] = part_ref[...]
    halo_wait(2, 2)
    add_rim(2, app_ref, 0, 0, 0)
    outer_halo(2, app_ref)
    gather_wait(1)
    sums = jnp.sum(gbuf[1], axis=0)
    rz_now = sums[0:1, 0:1] + rz_coarse
    step_len = rz_now / sums[1:2, 0:1]
    pressure = step_len * search
    res_ref[...] = res_ref[...] - step_len * app_ref[...]
    gather_send(2, total(res_ref[0:ROWS] * invm_ref[...]))

    local = local_solve() * invm_ref[...]
    part_ref[...] = fold_in(local)
    halo_send(3, 1)
    gather_send(3, total(res_ref[0:ROWS] * local))
    gather_wait(2)
    x, rz_coarse = coarse(gathered(2, 0))
    field = coarse_field(x)
    halo_wait(3, 1)
    add_rim(3, part_ref, 0, 0, 0)
    gather_wait(3)
    sums = jnp.sum(gbuf[3], axis=0)
    rz_next = sums[0:1, 0:1] + rz_coarse
    search = part_ref[...] + field + (rz_next / rz_now) * search_ref[...]

    applied = helm(search)
    gather_send(4, total(search * applied))
    gather_wait(4)
    sums = jnp.sum(gbuf[4], axis=0)
    pressure_out[...] = pressure + (rz_next / sums[0:1, 0:1]) * search

    for r, layers in enumerate((3, 1, 2, 1)):
        halo_drain(r, layers)
    for g in range(5):
        gather_bytes(g, gsend_sem.at[g])


def body(ngx, ngy, level_set, velocity, source, wick_solid):
    n = ngx * ngy
    npad = -(-n // 128) * 128
    consts = [jnp.asarray(t) for t in tables()]
    vmem = pl.BlockSpec(memory_space=pltpu.VMEM)
    shape = level_set.shape
    level_new, pressure = pl.pallas_call(
        functools.partial(kernel, ngx, ngy),
        out_shape=[jax.ShapeDtypeStruct((ROWS, 128), F32)] * 2,
        in_specs=[vmem] * (4 + len(consts)),
        out_specs=[vmem] * 2,
        scratch_shapes=[
            pltpu.VMEM((ROWS, 128), F32),
            pltpu.VMEM((ROWS, 128), F32),
            pltpu.VMEM((ROWS, 128), F32),
            pltpu.VMEM((ROWS, 128), F32),
            pltpu.VMEM((EXT, 128), F32),
            pltpu.VMEM((EXT, 128), F32),
            pltpu.VMEM((ROWS, 128), F32),
            pltpu.VMEM((n, npad), F32),
            pltpu.VMEM((4, 2, 96, 128), F32),
            pltpu.VMEM((4, 2, 96, 128), F32),
            pltpu.VMEM((4, 2, 24, 128), F32),
            pltpu.VMEM((4, 2, 24, 128), F32),
            pltpu.VMEM((4, 4, 8, 128), F32),
            pltpu.VMEM((4, 4, 8, 128), F32),
            pltpu.VMEM((5, n, 2, 128), F32),
            pltpu.SemaphoreType.DMA((4, 8)),
            pltpu.SemaphoreType.DMA((4, 8)),
            pltpu.SemaphoreType.DMA((5,)),
            pltpu.SemaphoreType.DMA((5,)),
        ],
        compiler_params=pltpu.CompilerParams(
            collective_id=0, has_side_effects=True, vmem_limit_bytes=48 * 1024 * 1024
        ),
    )(
        level_set.reshape(ROWS, 128),
        velocity.reshape(3 * ROWS, 128),
        source.reshape(ROWS, 128),
        wick_solid,
        *consts,
    )
    return level_new.reshape(shape), pressure.reshape(shape)


def solution(mesh):
    placed = (
        P("gx", "gy", None),
        P(None, "gx", "gy", None),
        P("gx", "gy", None),
        P("gx", "gy", None),
    )
    return jax.shard_map(
        functools.partial(body, mesh.shape["gx"], mesh.shape["gy"]),
        mesh=mesh,
        in_specs=placed,
        out_specs=(P("gx", "gy", None), P("gx", "gy", None)),
        check_vma=False,
    )
```

profile of v0, /device:TPU:0, one launch (start us, length us, event | category | flops | bytes accessed | tf_op | source)
XLA Modules:
  0.0 58.6 jit_solution(7969091519337740363)
XLA Ops:
  0.6 0.0 copy-start.21
  0.6 0.0 copy-start.22
  0.7 0.7 %copy-done.21 = f32[16,128]{1,0:T(8,128)S(1)} copy-done((f32[16,128]{1,0:T(8,128)S(1)}, f32[16,128]{1,0:T(8,128)}, u32[]{:S(2)}) %copy-start.21) | copy-done | bytes 8216
  1.3 0.0 copy-done.22
  1.3 0.0 copy-start
  1.3 1.0 %copy-done = f32[400,256]{1,0:T(8,128)S(1)} copy-done((f32[400,256]{1,0:T(8,128)S(1)}, f32[400,256]{1,0:T(8,128)}, u32[]{:S(2)}) %copy-start) | copy-done | bytes 409624
  2.3 0.0 copy-start.1
  2.3 1.0 %copy-done.1 = f32[3,8,32,128]{3,2,1,0:T(8,128)S(1)} copy-done((f32[3,8,32,128]{3,2,1,0:T(8,128)S(1)}, f32[3,8,32,128]{3,2,1,0:T(8,128)}, u32[]{:S(2)}) %copy-start.1) | copy-done | bytes 393240
  3.3 0.0 copy-start.2
  3.3 1.0 %copy-done.2 = bf16[400,384]{1,0:T(8,128)(2,1)S(1)} copy-done((bf16[400,384]{1,0:T(8,128)(2,1)S(1)}, bf16[400,384]{1,0:T(8,128)(2,1)}, u32[]{:S(2)}) %copy-start.2) | copy-done | bytes 307224
  4.3 0.0 copy-start.3
  4.3 1.0 %copy-done.3 = bf16[400,384]{1,0:T(8,128)(2,1)S(1)} copy-done((bf16[400,384]{1,0:T(8,128)(2,1)S(1)}, bf16[400,384]{1,0:T(8,128)(2,1)}, u32[]{:S(2)}) %copy-start.3) | copy-done | bytes 307224
  5.3 0.9 %copy-done.4 = bf16[256,400]{1,0:T(8,128)(2,1)S(1)} copy-done((bf16[256,400]{1,0:T(8,128)(2,1)S(1)}, bf16[256,400]{1,0:T(8,128)(2,1)}, u32[]{:S(2)}) %copy-start.4) | copy-done | bytes 204824
  6.2 0.9 %copy-done.5 = bf16[256,400]{1,0:T(8,128)(2,1)S(1)} copy-done((bf16[256,400]{1,0:T(8,128)(2,1)S(1)}, bf16[256,400]{1,0:T(8,128)(2,1)}, u32[]{:S(2)}) %copy-start.5) | copy-done | bytes 204824
  7.2 0.9 %copy-done.6 = bf16[256,512]{1,0:T(8,128)(2,1)S(1)} copy-done((bf16[256,512]{1,0:T(8,128)(2,1)S(1)}, bf16[256,512]{1,0:T(8,128)(2,1)}, u32[]{:S(2)}) %copy-start.6) | copy-done | bytes 262168
  8.1 0.9 %copy-done.7 = bf16[256,512]{1,0:T(8,128)(2,1)S(1)} copy-done((bf16[256,512]{1,0:T(8,128)(2,1)S(1)}, bf16[256,512]{1,0:T(8,128)(2,1)}, u32[]{:S(2)}) %copy-start.7) | copy-done | bytes 262168
  9.1 0.9 %copy-done.8 = bf16[512,256]{1,0:T(8,128)(2,1)S(1)} copy-done((bf16[512,256]{1,0:T(8,128)(2,1)S(1)}, bf16[512,256]{1,0:T(8,128)(2,1)}, u32[]{:S(2)}) %copy-start.8) | copy-done | bytes 262168
  10.0 0.9 %copy-done.9 = bf16[512,256]{1,0:T(8,128)(2,1)S(1)} copy-done((bf16[512,256]{1,0:T(8,128)(2,1)S(1)}, bf16[512,256]{1,0:T(8,128)(2,1)}, u32[]{:S(2)}) %copy-start.9) | copy-done | bytes 262168
  11.0 0.9 %copy-done.10 = f32[8,32,128]{2,1,0:T(8,128)S(1)} copy-done((f32[8,32,128]{2,1,0:T(8,128)S(1)}, f32[8,32,128]{2,1,0:T(8,128)}, u32[]{:S(2)}) %copy-start.10) | copy-done | bytes 131096
  11.9 0.9 %copy-done.11 = f32[8,32,128]{2,1,0:T(8,128)S(1)} copy-done((f32[8,32,128]{2,1,0:T(8,128)S(1)}, f32[8,32,128]{2,1,0:T(8,128)}, u32[]{:S(2)}) %copy-start.11) | copy-done | bytes 131096
  12.8 0.9 %copy-done.12 = f32[256,128]{1,0:T(8,128)S(1)} copy-done((f32[256,128]{1,0:T(8,128)S(1)}, f32[256,128]{1,0:T(8,128)}, u32[]{:S(2)}) %copy-start.12) | copy-done | bytes 131096
  13.7 0.8 %copy-done.13 = bf16[256,128]{1,0:T(8,128)(2,1)S(1)} copy-done((bf16[256,128]{1,0:T(8,128)(2,1)S(1)}, bf16[256,128]{1,0:T(8,128)(2,1)}, u32[]{:S(2)}) %copy-start.13) | copy-done | bytes 65560
  14.5 0.8 %copy-done.14 = bf16[256,128]{1,0:T(8,128)(2,1)S(1)} copy-done((bf16[256,128]{1,0:T(8,128)(2,1)S(1)}, bf16[256,128]{1,0:T(8,128)(2,1)}, u32[]{:S(2)}) %copy-start.14) | copy-done | bytes 65560
  15.4 0.8 %copy-done.15 = bf16[128,256]{1,0:T(8,128)(2,1)S(1)} copy-done((bf16[128,256]{1,0:T(8,128)(2,1)S(1)}, bf16[128,256]{1,0:T(8,128)(2,1)}, u32[]{:S(2)}) %copy-start.15) | copy-done | bytes 65560
  16.2 0.8 %copy-done.16 = bf16[128,256]{1,0:T(8,128)(2,1)S(1)} copy-done((bf16[128,256]{1,0:T(8,128)(2,1)S(1)}, bf16[128,256]{1,0:T(8,128)(2,1)}, u32[]{:S(2)}) %copy-start.16) | copy-done | bytes 65560
  17.0 0.8 %copy-done.17 = bf16[128,128]{1,0:T(8,128)(2,1)S(1)} copy-done((bf16[128,128]{1,0:T(8,128)(2,1)S(1)}, bf16[128,128]{1,0:T(8,128)(2,1)}, u32[]{:S(2)}) %copy-start.17) | copy-done | bytes 32792
  17.8 0.8 %copy-done.18 = bf16[128,128]{1,0:T(8,128)(2,1)S(1)} copy-done((bf16[128,128]{1,0:T(8,128)(2,1)S(1)}, bf16[128,128]{1,0:T(8,128)(2,1)}, u32[]{:S(2)}) %copy-start.18) | copy-done | bytes 32792
  18.6 0.8 %copy-done.19 = bf16[128,128]{1,0:T(8,128)(2,1)S(1)} copy-done((bf16[128,128]{1,0:T(8,128)(2,1)S(1)}, bf16[128,128]{1,0:T(8,128)(2,1)}, u32[]{:S(2)}) %copy-start.19) | copy-done | bytes 32792
  19.3 0.8 %copy-done.20 = bf16[128,128]{1,0:T(8,128)(2,1)S(1)} copy-done((bf16[128,128]{1,0:T(8,128)(2,1)S(1)}, bf16[128,128]{1,0:T(8,128)(2,1)}, u32[]{:S(2)}) %copy-start.20) | copy-done | bytes 32792
  20.1 37.2 %shard_map.230 = (f32[256,128]{1,0:T(8,128)S(1)}, f32[256,128]{1,0:T(8,128)S(1)}) custom-call(f32[256,128]{1,0:T(8,128)S(1)} %bitcast.6, f32[768,128]{1,0:T(8,128)S(1)} %bitcast.5, f32[256,128]{1,0:T(8,128)S(1)} %bitcast.7, s32[1,4,16]{2,1,0:T(4,128)S(1)} %copy-done.22, bf16[512,256]{1,0:T(8,128)(2,1)S(1)} %copy-done.9, bf16[512,256]{1,0:T(8,128)(2,1)S(1)} %copy-done.8, ...), custom_call_target="tpu_custom_call" | custom-call | tf_op jit(solution)/shard_map/pallas_call | solution.py:527
  57.3 0.7 %copy.27 = f32[8,32,128]{2,1,0:T(8,128)} copy(f32[8,32,128]{2,1,0:T(8,128)S(1)} %bitcast.9) | data formatting | bytes 262144
  58.0 0.7 %copy.28 = f32[8,32,128]{2,1,0:T(8,128)} copy(f32[8,32,128]{2,1,0:T(8,128)S(1)} %bitcast.8) | data formatting | bytes 262144
  (17 shorter events, 0.0 us)
Async XLA Ops:
  0.6 0.7 %copy-start.21 = (f32[16,128]{1,0:T(8,128)S(1)}, f32[16,128]{1,0:T(8,128)}, u32[]{:S(2)}) copy-start(f32[16,128]{1,0:T(8,128)} %constant.56.clone.spread_ref) | copy-start | bytes 24580
  0.6 0.7 %copy-start.22 = (s32[1,4,16]{2,1,0:T(4,128)S(1)}, s32[1,4,16]{2,1,0:T(4,128)}, u32[]{:S(2)}) copy-start(s32[1,4,16]{2,1,0:T(4,128)} %solid_ref.1) | copy-start | bytes 772
  1.3 1.0 %copy-start = (f32[400,256]{1,0:T(8,128)S(1)}, f32[400,256]{1,0:T(8,128)}, u32[]{:S(2)}) copy-start(f32[400,256]{1,0:T(8,128)} %constant.54.clone.inv_den_ref) | copy-start | bytes 1228804
  2.3 1.0 %copy-start.1 = (f32[3,8,32,128]{3,2,1,0:T(8,128)S(1)}, f32[3,8,32,128]{3,2,1,0:T(8,128)}, u32[]{:S(2)}) copy-start(f32[3,8,32,128]{3,2,1,0:T(8,128)} %param.24) | copy-start | bytes 1179652
  3.3 1.0 %copy-start.2 = (bf16[400,384]{1,0:T(8,128)(2,1)S(1)}, bf16[400,384]{1,0:T(8,128)(2,1)}, u32[]{:S(2)}) copy-start(bf16[400,384]{1,0:T(8,128)(2,1)} %constant.47.clone.szl) | copy-start | bytes 921604
  4.3 1.0 %copy-start.3 = (bf16[400,384]{1,0:T(8,128)(2,1)S(1)}, bf16[400,384]{1,0:T(8,128)(2,1)}, u32[]{:S(2)}) copy-start(bf16[400,384]{1,0:T(8,128)(2,1)} %constant.46.clone.szh) | copy-start | bytes 921604
  5.3 0.9 %copy-start.4 = (bf16[256,400]{1,0:T(8,128)(2,1)S(1)}, bf16[256,400]{1,0:T(8,128)(2,1)}, u32[]{:S(2)}) copy-start(bf16[256,400]{1,0:T(8,128)(2,1)} %constant.51.clone.bzl) | copy-start | bytes 614404
  6.2 0.9 %copy-start.5 = (bf16[256,400]{1,0:T(8,128)(2,1)S(1)}, bf16[256,400]{1,0:T(8,128)(2,1)}, u32[]{:S(2)}) copy-start(bf16[256,400]{1,0:T(8,128)(2,1)} %constant.50.clone.bzh) | copy-start | bytes 614404
  7.2 0.9 %copy-start.6 = (bf16[256,512]{1,0:T(8,128)(2,1)S(1)}, bf16[256,512]{1,0:T(8,128)(2,1)}, u32[]{:S(2)}) copy-start(bf16[256,512]{1,0:T(8,128)(2,1)} %constant.41.clone.gtl) | copy-start | bytes 786436
  8.1 0.9 %copy-start.7 = (bf16[256,512]{1,0:T(8,128)(2,1)S(1)}, bf16[256,512]{1,0:T(8,128)(2,1)}, u32[]{:S(2)}) copy-start(bf16[256,512]{1,0:T(8,128)(2,1)} %constant.40.clone.gth) | copy-start | bytes 786436
  9.1 0.9 %copy-start.8 = (bf16[512,256]{1,0:T(8,128)(2,1)S(1)}, bf16[512,256]{1,0:T(8,128)(2,1)}, u32[]{:S(2)}) copy-start(bf16[512,256]{1,0:T(8,128)(2,1)} %constant.39.clone.gl) | copy-start | bytes 786436
  10.0 0.9 %copy-start.9 = (bf16[512,256]{1,0:T(8,128)(2,1)S(1)}, bf16[512,256]{1,0:T(8,128)(2,1)}, u32[]{:S(2)}) copy-start(bf16[512,256]{1,0:T(8,128)(2,1)} %constant.38.clone.gh) | copy-start | bytes 786436
  11.0 0.9 %copy-start.10 = (f32[8,32,128]{2,1,0:T(8,128)S(1)}, f32[8,32,128]{2,1,0:T(8,128)}, u32[]{:S(2)}) copy-start(f32[8,32,128]{2,1,0:T(8,128)} %param.23) | copy-start | bytes 393220
  11.9 0.9 %copy-start.11 = (f32[8,32,128]{2,1,0:T(8,128)S(1)}, f32[8,32,128]{2,1,0:T(8,128)}, u32[]{:S(2)}) copy-start(f32[8,32,128]{2,1,0:T(8,128)} %param.25) | copy-start | bytes 393220
  12.8 0.9 %copy-start.12 = (f32[256,128]{1,0:T(8,128)S(1)}, f32[256,128]{1,0:T(8,128)}, u32[]{:S(2)}) copy-start(f32[256,128]{1,0:T(8,128)} %constant.55.clone.mass_ref) | copy-start | bytes 393220
  13.7 0.8 %copy-start.13 = (bf16[256,128]{1,0:T(8,128)(2,1)S(1)}, bf16[256,128]{1,0:T(8,128)(2,1)}, u32[]{:S(2)}) copy-start(bf16[256,128]{1,0:T(8,128)(2,1)} %constant.53.clone.bxl) | copy-start | bytes 196612
  14.5 0.8 %copy-start.14 = (bf16[256,128]{1,0:T(8,128)(2,1)S(1)}, bf16[256,128]{1,0:T(8,128)(2,1)}, u32[]{:S(2)}) copy-start(bf16[256,128]{1,0:T(8,128)(2,1)} %constant.52.clone.bxh) | copy-start | bytes 196612
  15.4 0.8 %copy-start.15 = (bf16[128,256]{1,0:T(8,128)(2,1)S(1)}, bf16[128,256]{1,0:T(8,128)(2,1)}, u32[]{:S(2)}) copy-start(bf16[128,256]{1,0:T(8,128)(2,1)} %constant.49.clone.sxl) | copy-start | bytes 196612
  16.2 0.8 %copy-start.16 = (bf16[128,256]{1,0:T(8,128)(2,1)S(1)}, bf16[128,256]{1,0:T(8,128)(2,1)}, u32[]{:S(2)}) copy-start(bf16[128,256]{1,0:T(8,128)(2,1)} %constant.48.clone.sxh) | copy-start | bytes 196612
  17.0 0.8 %copy-start.17 = (bf16[128,128]{1,0:T(8,128)(2,1)S(1)}, bf16[128,128]{1,0:T(8,128)(2,1)}, u32[]{:S(2)}) copy-start(bf16[128,128]{1,0:T(8,128)(2,1)} %constant.45.clone.dxl) | copy-start | bytes 98308
  17.8 0.8 %copy-start.18 = (bf16[128,128]{1,0:T(8,128)(2,1)S(1)}, bf16[128,128]{1,0:T(8,128)(2,1)}, u32[]{:S(2)}) copy-start(bf16[128,128]{1,0:T(8,128)(2,1)} %constant.44.clone.dxh) | copy-start | bytes 98308
  18.6 0.8 %copy-start.19 = (bf16[128,128]{1,0:T(8,128)(2,1)S(1)}, bf16[128,128]{1,0:T(8,128)(2,1)}, u32[]{:S(2)}) copy-start(bf16[128,128]{1,0:T(8,128)(2,1)} %constant.43.clone.dxtl) | copy-start | bytes 98308
  19.3 0.8 %copy-start.20 = (bf16[128,128]{1,0:T(8,128)(2,1)S(1)}, bf16[128,128]{1,0:T(8,128)(2,1)}, u32[]{:S(2)}) copy-start(bf16[128,128]{1,0:T(8,128)(2,1)} %constant.42.clone.dxth) | copy-start | bytes 98308
where the time goes:
time: 59.7 us; the launch traced here: 58.6 us
  Pallas kernels  37.2 us (62%)
  local copies, waits for them, and re-layouts  20.7 us (35%)
  between operations  0.68 us (1%)
    pallas_call x1, Pallas kernels, body(): pl.pallas_call(functools.partial(kernel, ngx, ngy), out_shape=[jax.ShapeD...  37.2 us
    unnamed x48, local copies, waits for them, and re-layouts  20.7 us

commit v1 on v0

--- a/solution.py
+++ b/solution.py
@@ -25,6 +25,7 @@
 SCHWARZ_SHIFT = 0.05
 
 MESH = pl.DeviceIdType.MESH
+LOGICAL = pl.DeviceIdType.LOGICAL
 F32 = jnp.float32
 BF16 = jnp.bfloat16
 
@@ -81,9 +82,7 @@
     ids = np.arange(10) + 1.0
     sine = np.sqrt(2.0 / 11.0) * np.sin(np.pi * np.outer(ids, ids) / 11.0)
     eig = 2.0 - 2.0 * np.cos(np.pi * ids / 11.0)
-    dz = np.kron(deriv, np.eye(32))
     dy = np.kron(np.eye(32), deriv)
-    grad = np.concatenate([dz, dy], axis=0)
     dx_t = np.kron(np.eye(EX), deriv.T)
     dx = np.kron(np.eye(EX), deriv)
 
@@ -124,12 +123,20 @@
     mass = 0.125 * (
         np.kron(weight, np.tile(weight, EY))[:, None] * np.tile(weight, EX)[None, :]
     )
-    out = []
-    for table in (grad, grad.T, dx_t, dx, spec_zy, spec_x, back_zy, back_x):
-        out.extend(halves(table))
-    spread = np.kron(np.eye(EX), np.ones((1, 8)))
-    out += [inv_den.astype(np.float32), mass.astype(np.float32), spread.astype(np.float32)]
-    return out
+    spread = np.zeros((16, 128))
+    spread[:EX] = np.kron(np.eye(EX), np.ones((1, 8)))
+
+    def stack(*parts):
+        return np.concatenate([half for part in parts for half in halves(part)], axis=0)
+
+    return (
+        stack(dy, dy.T, spec_x),
+        stack(dx_t, dx, back_x),
+        np.concatenate([mass, spread], axis=0).astype(np.float32),
+        stack(spec_zy),
+        inv_den.astype(np.float32),
+        stack(back_zy),
+    )
 
 
 def split(v):
@@ -142,16 +149,32 @@
     return jnp.dot(a, b, preferred_element_type=F32)
 
 
-def left(high_ref, low_ref, v, rows=None):
-    pick = slice(None) if rows is None else rows
+def left(ref, base, rows, v):
     vh, vl = split(v)
-    both = dot(high_ref[pick, :], jnp.concatenate([vh, vl], axis=1))
-    return both[:, :128] + both[:, 128:] + dot(low_ref[pick, :], vh)
-
-
-def right(v, high_ref, low_ref):
+    both = dot(ref[base : base + rows, :], jnp.concatenate([vh, vl], axis=1))
+    return both[:, :128] + both[:, 128:] + dot(ref[base + rows : base + 2 * rows, :], vh)
+
+
+def right(v, ref, base, rows):
     vh, vl = split(v)
-    return dot(vh, high_ref[...]) + dot(vl, high_ref[...]) + dot(vh, low_ref[...])
+    high = ref[base : base + rows, :]
+    return dot(vh, high) + dot(vl, high) + dot(vh, ref[base + rows : base + 2 * rows, :])
+
+
+def along_z(v, table):
+    planes = [v[32 * i : 32 * i + 32] for i in range(8)]
+    even = [planes[j] + planes[7 - j] for j in range(4)]
+    odd = [planes[j] - planes[7 - j] for j in range(4)]
+    low, high = [], []
+    for i in range(4):
+        a = b = None
+        for j in range(4):
+            p = float(table[i, j] + table[i, 7 - j]) / 2.0 * even[j]
+            q = float(table[i, j] - table[i, 7 - j]) / 2.0 * odd[j]
+            a, b = (p, q) if a is None else (a + p, b + q)
+        low.append(a + b)
+        high.insert(0, b - a)
+    return jnp.concatenate(low + high, axis=0)
 
 
 def total(v):
@@ -166,20 +189,39 @@
 
 
 def kernel(
-    ngx, ngy,
-    level_ref, vel_ref, source_ref, solid_ref,
-    gh, gl, gth, gtl, dxth, dxtl, dxh, dxl, szh, szl, sxh, sxl, bzh, bzl, bxh, bxl,
-    inv_den_ref, mass_ref, spread_ref,
-    level_out, pressure_out,
-    flux_ref, invm_ref, part_ref, lev_ref, app_ref, res_ref, search_ref, a_ref,
-    zs, zr, ys, yr, cs, cr, gbuf,
-    send_sem, recv_sem, gsend_sem, grecv_sem,
+    ngx, ngy, deriv,
+    level_hbm, vel_hbm, source_hbm, solid_hbm, *refs
 ):
+    tables_hbm, refs = refs[:6], refs[6:]
+    level_out, pressure_out = refs[:2]
+    (
+        flux_ref, invm_ref, part_ref, lev_ref, app_ref, res_ref, search_ref, a_ref,
+        zs, zr, ys, yr, cs, cr, gbuf,
+        level_ref, vel_ref, source_ref, solid_ref,
+        t256, t128, mass_ref, spec_ref, den_ref, back_ref,
+        send_sem, recv_sem, gsend_sem, grecv_sem, load_sem,
+    ) = refs[2:]
+    loads = [
+        pltpu.make_async_copy(src, dst, load_sem.at[i])
+        for i, (src, dst) in enumerate(
+            zip(
+                (level_hbm, vel_hbm, source_hbm, solid_hbm) + tables_hbm,
+                (level_ref, vel_ref, source_ref, solid_ref)
+                + (t256, t128, mass_ref, spec_ref, den_ref, back_ref),
+            )
+        )
+    ]
+    for i in (4, 5, 0, 1, 6, 2, 3, 7, 8, 9):
+        loads[i].start()
     n = ngx * ngy
     ix = lax.axis_index("gx")
     iy = lax.axis_index("gy")
     me = ix * ngy + iy
 
+    def other(i):
+        at = me + i
+        return jnp.where(at >= n, at - n, at)
+
     zr[...] = jnp.zeros_like(zr)
     yr[...] = jnp.zeros_like(yr)
     cr[...] = jnp.zeros_like(cr)
@@ -187,13 +229,10 @@
     barrier = pltpu.get_barrier_semaphore()
 
     def greet(i, carry):
-        dst = lax.rem(me + i, n)
-        pl.semaphore_signal(
-            barrier, inc=1, device_id=(dst // ngy, lax.rem(dst, ngy)), device_id_type=MESH
-        )
+        pl.semaphore_signal(barrier, inc=1, device_id=other(i), device_id_type=LOGICAL)
         return carry
 
-    lax.fori_loop(1, n, greet, 0)
+    lax.fori_loop(1, n, greet, 0, unroll=n <= 64)
 
     has_zlo, has_zhi = ix > 0, ix < ngx - 1
     has_ylo, has_yhi = iy > 0, iy < ngy - 1
@@ -311,8 +350,8 @@
             dst_ref=gbuf.at[g, me],
             send_sem=gsend_sem.at[g],
             recv_sem=grecv_sem.at[g],
-            device_id=(dst // ngy, lax.rem(dst, ngy)),
-            device_id_type=MESH,
+            device_id=dst,
+            device_id_type=LOGICAL,
         )
 
     def gather_send(g, first, second=None):
@@ -321,10 +360,10 @@
             gbuf[g, me, 1:2] = jnp.broadcast_to(second, (1, 128))
 
         def send(i, carry):
-            gather_copy(g, lax.rem(me + i, n)).start()
+            gather_copy(g, other(i)).start()
             return carry
 
-        lax.fori_loop(1, n, send, 0)
+        lax.fori_loop(1, n, send, 0, unroll=n <= 64)
 
     def gather_bytes(g, sem):
         ref = gbuf.at[g, pl.ds(0, n - 1)]
@@ -362,26 +401,29 @@
         v = v + x_first * pltpu.roll(v, 1, 1) + x_last * pltpu.roll(v, 127, 1)
         return v + y_first * pltpu.roll(v, 1, 0) + y_last * pltpu.roll(v, ROWS - 1, 0)
 
-    mass = mass_ref[...]
+    for i in (4, 5, 0, 1, 6):
+        loads[i].wait()
+    mass = mass_ref[0:ROWS]
     level = level_ref[...]
-    grads = left(gh, gl, level)
     advect = (
-        vel_ref[0:ROWS] * grads[:ROWS]
-        + vel_ref[ROWS : 2 * ROWS] * grads[ROWS:]
-        + vel_ref[2 * ROWS : 3 * ROWS] * right(level, dxth, dxtl)
+        vel_ref[0:ROWS] * along_z(level, deriv)
+        + vel_ref[ROWS : 2 * ROWS] * left(t256, 0, ROWS, level)
+        + vel_ref[2 * ROWS : 3 * ROWS] * right(level, t128, 0, 128)
     )
     lev_ref[...] = fold_in(mass * (level - (2.0 * TIME_STEP) * advect))
     diverge = (
-        left(gh, gl, vel_ref[0:ROWS], slice(0, ROWS))
-        + left(gh, gl, vel_ref[ROWS : 2 * ROWS], slice(ROWS, 2 * ROWS))
-        + right(vel_ref[2 * ROWS : 3 * ROWS], dxth, dxtl)
-    )
+        along_z(vel_ref[0:ROWS], deriv)
+        + left(t256, 0, ROWS, vel_ref[ROWS : 2 * ROWS])
+        + right(vel_ref[2 * ROWS : 3 * ROWS], t128, 0, 128)
+    )
+    loads[2].wait()
     part_ref[...] = fold_in(mass * (source_ref[...] - (2.0 * TIME_STEP) * diverge))
 
     pl.semaphore_wait(barrier, n - 1)
     halo_send(0, 3, lev_ref)
     res_ref[0:ROWS] = part_ref[...]
-    solid = dot(solid_ref[0].astype(F32), spread_ref[...])
+    loads[3].wait()
+    solid = dot(solid_ref[0].astype(F32), mass_ref[ROWS : ROWS + EX])
     solid = jnp.concatenate(
         [jnp.broadcast_to(solid[e : e + 1], (8, 128)) for e in range(EY)], axis=0
     )
@@ -399,15 +441,16 @@
     gather_send(0, total(coef) / (ROWS * 128.0), total(res_ref[0:ROWS] * inv_m))
 
     def local_solve():
-        spectral = right(left(szh, szl, res_ref[...]), sxh, sxl) * inv_den_ref[...]
-        return left(bzh, bzl, right(spectral, bxh, bxl))
+        spectral = right(left(spec_ref, 0, SPEC, res_ref[...]), t256, 4 * ROWS, 128)
+        spectral = spectral * den_ref[...]
+        return left(back_ref, 0, ROWS, right(spectral, t128, 512, 256))
 
     def helm(v):
-        grads = left(gh, gl, v)
         flux = flux_ref[...]
-        out = left(gth, gtl, jnp.concatenate([flux * grads[:ROWS], flux * grads[ROWS:]], axis=0))
-        out = out + right(flux * right(v, dxth, dxtl), dxh, dxl)
-        return out + HELM_COEF * mass_ref[...] * v
+        out = along_z(flux * along_z(v, deriv), deriv.T)
+        out = out + left(t256, 2 * ROWS, ROWS, flux * left(t256, 0, ROWS, v))
+        out = out + right(flux * right(v, t128, 0, 128), t128, 256, 128)
+        return out + HELM_COEF * mass_ref[0:ROWS] * v
 
     npad = a_ref.shape[1]
     sub_n = lax.broadcasted_iota(jnp.int32, (n, npad), 0)
@@ -433,7 +476,11 @@
         a = jnp.where(diag, diagonal, -link)
         if n <= 64:
             for k in range(n):
-                a = sweep_step(a, a[k : k + 1, :], a[:, k : k + 1], k, sub_n, lane_n)
+                col = jnp.broadcast_to(a[:, k : k + 1], (n, npad))
+                row_m = jnp.where(lane_n[:1] == k, -1.0, a[k : k + 1, :]) / col[k : k + 1, :]
+                col_m = jnp.where(sub_n == k, -1.0, col)
+                cross = jnp.logical_or(lane_n == k, sub_n == k)
+                a = jnp.where(cross, 0.0, a) - col_m * row_m
             a_ref[...] = a
         else:
             a_ref[...] = a
@@ -462,6 +509,8 @@
 
         return own_z * along_y(0) + half_zlo * along_y(-1) + half_zhi * along_y(1)
 
+    for i in (7, 8, 9):
+        loads[i].wait()
     local = local_solve() * inv_m
     part_ref[...] = fold_in(local)
     halo_send(1, 1)
@@ -522,12 +571,13 @@
     n = ngx * ngy
     npad = -(-n // 128) * 128
     consts = [jnp.asarray(t) for t in tables()]
+    hbm = pl.BlockSpec(memory_space=pltpu.HBM)
     vmem = pl.BlockSpec(memory_space=pltpu.VMEM)
     shape = level_set.shape
     level_new, pressure = pl.pallas_call(
-        functools.partial(kernel, ngx, ngy),
+        functools.partial(kernel, ngx, ngy, gll_tables()[1]),
         out_shape=[jax.ShapeDtypeStruct((ROWS, 128), F32)] * 2,
-        in_specs=[vmem] * (4 + len(consts)),
+        in_specs=[hbm] * (4 + len(consts)),
         out_specs=[vmem] * 2,
         scratch_shapes=[
             pltpu.VMEM((ROWS, 128), F32),
@@ -545,13 +595,19 @@
             pltpu.VMEM((4, 4, 8, 128), F32),
             pltpu.VMEM((4, 4, 8, 128), F32),
             pltpu.VMEM((5, n, 2, 128), F32),
+            pltpu.VMEM((ROWS, 128), F32),
+            pltpu.VMEM((3 * ROWS, 128), F32),
+            pltpu.VMEM((ROWS, 128), F32),
+            pltpu.VMEM((1, EY, EX), jnp.int32),
+            *[pltpu.VMEM(t.shape, t.dtype) for t in consts],
             pltpu.SemaphoreType.DMA((4, 8)),
             pltpu.SemaphoreType.DMA((4, 8)),
             pltpu.SemaphoreType.DMA((5,)),
             pltpu.SemaphoreType.DMA((5,)),
+            pltpu.SemaphoreType.DMA((10,)),
         ],
         compiler_params=pltpu.CompilerParams(
-            collective_id=0, has_side_effects=True, vmem_limit_bytes=48 * 1024 * 1024
+            collective_id=0, has_side_effects=True, vmem_limit_bytes=63 * 1024 * 1024
         ),
     )(
         level_set.reshape(ROWS, 128),

time: 59.7 us -> 39.2 us (0.66); the launches traced: 58.6 us -> 39 us
  local copies, waits for them, and re-layouts: 20.7 us -> 2.26 us
  Pallas kernels: 37.2 us -> 36.1 us
    unnamed x48 -> x4, local copies, waits for them, and re-layouts: 20.7 us -> 2.26 us
    pallas_call x1, Pallas kernels: 37.2 us -> 36.1 us  [body(): pl.pallas_call(functools.partial(kernel, ngx, ngy, gll_tables()[1]), out_...]
where the time goes in v1:
time: 39.2 us; the launch traced here: 39 us
  Pallas kernels  36.1 us (92%)
  local copies, waits for them, and re-layouts  2.26 us (6%)
  between operations  0.65 us (2%)
    pallas_call x1, Pallas kernels, body(): pl.pallas_call(functools.partial(kernel, ngx, ngy, gll_tables()[1]), out_...  36.1 us
    unnamed x4, local copies, waits for them, and re-layouts  2.26 us

profile of v1, /device:TPU:0, one launch (start us, length us, event | category | flops | bytes accessed | tf_op | source)
XLA Modules:
  0.0 39.0 jit_solution(17903901249992633422)
XLA Ops:
  0.6 36.1 %shard_map.113 = (f32[256,128]{1,0:T(8,128)}, f32[256,128]{1,0:T(8,128)}) custom-call(f32[256,128]{1,0:T(8,128)} %bitcast.6, f32[768,128]{1,0:T(8,128)} %bitcast.5, f32[256,128]{1,0:T(8,128)} %bitcast.7, s32[1,4,16]{2,1,0:T(4,128)} %solid_hbm.1, bf16[1280,256]{1,0:T(8,128)(2,1)} %constant.12.clone.refs_0_, bf16[1024,128]{1,0:T(8,128)(2,1)} %constant.13.clone.refs_1_, ...), custom_call_target="tpu_custom_call" | custom-call | tf_op jit(solution)/shard_map/pallas_call | solution.py:577
  36.7 0.0 copy-start
  36.8 1.6 %copy.14 = f32[8,32,128]{2,1,0:T(8,128)} copy(f32[8,32,128]{2,1,0:T(8,128)} %bitcast.9) | data formatting | bytes 262144
  38.4 0.0 copy-done
  38.4 0.7 %copy.15 = f32[8,32,128]{2,1,0:T(8,128)} copy(f32[8,32,128]{2,1,0:T(8,128)S(1)} %bitcast.8) | data formatting | bytes 262144
Async XLA Ops:
  36.7 1.6 %copy-start = (f32[256,128]{1,0:T(8,128)S(1)}, f32[256,128]{1,0:T(8,128)}, u32[]{:S(2)}) copy-start(f32[256,128]{1,0:T(8,128)} %get-tuple-element.5) | copy-start | bytes 393220

commit v2 on v1

--- a/solution.py
+++ b/solution.py
@@ -196,7 +196,7 @@
     level_out, pressure_out = refs[:2]
     (
         flux_ref, invm_ref, part_ref, lev_ref, app_ref, res_ref, search_ref, a_ref,
-        zs, zr, ys, yr, cs, cr, gbuf,
+        zs, zr, ys, yr, cs, cr, gbuf0, gbuf1, gbuf2,
         level_ref, vel_ref, source_ref, solid_ref,
         t256, t128, mass_ref, spec_ref, den_ref, back_ref,
         send_sem, recv_sem, gsend_sem, grecv_sem, load_sem,
@@ -213,6 +213,7 @@
     ]
     for i in (4, 5, 0, 1, 6, 2, 3, 7, 8, 9):
         loads[i].start()
+    gbufs = (gbuf0, gbuf1, gbuf2)
     n = ngx * ngy
     ix = lax.axis_index("gx")
     iy = lax.axis_index("gy")
@@ -345,19 +346,19 @@
             ref[336 + c : 337 + c] = cr[r, c, 3:4]
 
     def gather_copy(g, dst):
+        ref = gbufs[g].at[me]
         return pltpu.make_async_remote_copy(
-            src_ref=gbuf.at[g, me],
-            dst_ref=gbuf.at[g, me],
+            src_ref=ref,
+            dst_ref=ref,
             send_sem=gsend_sem.at[g],
             recv_sem=grecv_sem.at[g],
             device_id=dst,
             device_id_type=LOGICAL,
         )
 
-    def gather_send(g, first, second=None):
-        gbuf[g, me, 0:1] = jnp.broadcast_to(first, (1, 128))
-        if second is not None:
-            gbuf[g, me, 1:2] = jnp.broadcast_to(second, (1, 128))
+    def gather_send(g, rows):
+        for k, value in enumerate(rows):
+            gbufs[g][me, k : k + 1] = jnp.broadcast_to(value, (1, 128))
 
         def send(i, carry):
             gather_copy(g, other(i)).start()
@@ -366,7 +367,7 @@
         lax.fori_loop(1, n, send, 0, unroll=n <= 64)
 
     def gather_bytes(g, sem):
-        ref = gbuf.at[g, pl.ds(0, n - 1)]
+        ref = gbufs[g].at[pl.ds(0, n - 1)]
         pltpu.make_async_copy(ref, ref, sem).wait()
 
     def gather_wait(g):
@@ -438,10 +439,10 @@
         1.0 - (1.0 - SOLID_FACTOR) * solid
     )
     flux_ref[...] = 4.0 * coef * mass
-    gather_send(0, total(coef) / (ROWS * 128.0), total(res_ref[0:ROWS] * inv_m))
-
-    def local_solve():
-        spectral = right(left(spec_ref, 0, SPEC, res_ref[...]), t256, 4 * ROWS, 128)
+    gather_send(0, (total(coef) / (ROWS * 128.0), total(res_ref[0:ROWS] * inv_m)))
+
+    def local_solve(ref):
+        spectral = right(left(spec_ref, 0, SPEC, ref[...]), t256, 4 * ROWS, 128)
         spectral = spectral * den_ref[...]
         return left(back_ref, 0, ROWS, right(spectral, t128, 512, 256))
 
@@ -457,7 +458,7 @@
     lane_n = lax.broadcasted_iota(jnp.int32, (n, npad), 1)
 
     def gathered(g, item):
-        got = gbuf[g, :, item, :]
+        got = gbufs[g][:, item, :]
         return got if npad == 128 else jnp.concatenate([got] * (npad // 128), axis=1)
 
     def invert(k_col):
@@ -474,13 +475,22 @@
         link = 2.0 * k_col * k_row / (k_col + k_row) * rate
         diagonal = HELM_COEF * EZ * EY * EX + jnp.sum(link, axis=1, keepdims=True)
         a = jnp.where(diag, diagonal, -link)
-        if n <= 64:
-            for k in range(n):
-                col = jnp.broadcast_to(a[:, k : k + 1], (n, npad))
-                row_m = jnp.where(lane_n[:1] == k, -1.0, a[k : k + 1, :]) / col[k : k + 1, :]
-                col_m = jnp.where(sub_n == k, -1.0, col)
-                cross = jnp.logical_or(lane_n == k, sub_n == k)
-                a = jnp.where(cross, 0.0, a) - col_m * row_m
+        if n <= 64 and n % 2 == 0:
+            for k in range(0, n, 2):
+                c1 = jnp.broadcast_to(a[:, k : k + 1], (n, npad))
+                c2 = jnp.broadcast_to(a[:, k + 1 : k + 2], (n, npad))
+                p11, p12, p22 = c1[k : k + 1], c2[k : k + 1], c2[k + 1 : k + 2]
+                scale = 1.0 / (p11 * p22 - p12 * p12)
+                at1, at2 = lane_n == k, lane_n == k + 1
+                on1, on2 = sub_n == k, sub_n == k + 1
+                r1 = jnp.where(at1[:1], -1.0, jnp.where(at2[:1], 0.0, a[k : k + 1]))
+                r2 = jnp.where(at2[:1], -1.0, jnp.where(at1[:1], 0.0, a[k + 1 : k + 2]))
+                q1 = (p22 * r1 - p12 * r2) * scale
+                q2 = (p11 * r2 - p12 * r1) * scale
+                c1 = jnp.where(on1, -1.0, jnp.where(on2, 0.0, c1))
+                c2 = jnp.where(on2, -1.0, jnp.where(on1, 0.0, c2))
+                cross = jnp.logical_or(jnp.logical_or(at1, at2), jnp.logical_or(on1, on2))
+                a = jnp.where(cross, 0.0, a) - c1 * q1 - c2 * q2
             a_ref[...] = a
         else:
             a_ref[...] = a
@@ -495,9 +505,7 @@
             lax.fori_loop(0, n, step, 0)
 
     def coarse(t_col):
-        x = -jnp.sum(a_ref[...] * t_col, axis=0, keepdims=True)
-        t_row = jnp.sum(jnp.where(lane_n == sub_n, t_col, 0.0), axis=0, keepdims=True)
-        return x, jnp.sum(x * t_row, axis=1, keepdims=True)
+        return -jnp.sum(a_ref[...] * t_col, axis=0, keepdims=True)
 
     def coarse_field(x):
         def value(dz, dy):
@@ -509,61 +517,62 @@
 
         return own_z * along_y(0) + half_zlo * along_y(-1) + half_zhi * along_y(1)
 
+    def rows_sum(v):
+        return jnp.sum(v, axis=0, keepdims=True)
+
     for i in (7, 8, 9):
         loads[i].wait()
-    local = local_solve() * inv_m
-    part_ref[...] = fold_in(local)
+    part_ref[...] = fold_in(local_solve(res_ref) * inv_m)
     halo_send(1, 1)
-    rz_part = total(res_ref[0:ROWS] * local)
     gather_wait(0)
     invert(gathered(0, 0))
-    x, rz_coarse = coarse(gathered(0, 1))
-    field = coarse_field(x)
+    field = coarse_field(coarse(gathered(0, 1)))
     halo_wait(1, 1)
     search_ref[...] = part_ref[...]
     add_rim(1, search_ref, 0, 0, 0)
-    search = search_ref[...] + field
-    search_ref[...] = search
-
-    applied = helm(search)
-    gather_send(1, rz_part, total(search * applied))
+    z1 = search_ref[...] + field
+    search_ref[...] = z1
+
+    applied = helm(z1)
     part_ref[...] = fold_in(applied)
     halo_send(2, 2)
+    sum_rz = rows_sum(res_ref[0:ROWS] * z1 * inv_m)
+    sum_za = rows_sum(z1 * applied)
     app_ref[0:ROWS] = part_ref[...]
     halo_wait(2, 2)
     add_rim(2, app_ref, 0, 0, 0)
     outer_halo(2, app_ref)
+    gather_send(1, (total(app_ref[0:ROWS] * invm_ref[...]),))
+
+    part_ref[...] = fold_in(local_solve(app_ref) * invm_ref[...])
+    halo_send(3, 1)
     gather_wait(1)
-    sums = jnp.sum(gbuf[1], axis=0)
-    rz_now = sums[0:1, 0:1] + rz_coarse
-    step_len = rz_now / sums[1:2, 0:1]
-    pressure = step_len * search
-    res_ref[...] = res_ref[...] - step_len * app_ref[...]
-    gather_send(2, total(res_ref[0:ROWS] * invm_ref[...]))
-
-    local = local_solve() * invm_ref[...]
-    part_ref[...] = fold_in(local)
-    halo_send(3, 1)
-    gather_send(3, total(res_ref[0:ROWS] * local))
-    gather_wait(2)
-    x, rz_coarse = coarse(gathered(2, 0))
-    field = coarse_field(x)
+    field = coarse_field(coarse(gathered(1, 0)))
     halo_wait(3, 1)
     add_rim(3, part_ref, 0, 0, 0)
-    gather_wait(3)
-    sums = jnp.sum(gbuf[3], axis=0)
-    rz_next = sums[0:1, 0:1] + rz_coarse
-    search = part_ref[...] + field + (rz_next / rz_now) * search_ref[...]
-
-    applied = helm(search)
-    gather_send(4, total(search * applied))
-    gather_wait(4)
-    sums = jnp.sum(gbuf[4], axis=0)
-    pressure_out[...] = pressure + (rz_next / sums[0:1, 0:1]) * search
+    q = part_ref[...] + field
+
+    q_m = q * invm_ref[...]
+    gz, gy, gx = along_z(q, deriv), left(t256, 0, ROWS, q), right(q, t128, 0, 128)
+    energy = flux_ref[...] * (gz * gz + gy * gy + gx * gx)
+    energy = energy + HELM_COEF * mass_ref[0:ROWS] * (q * q)
+    sum_rq = rows_sum(res_ref[0:ROWS] * q_m)
+    sum_aq = rows_sum(app_ref[0:ROWS] * q_m)
+    gather_send(2, (sum_rz, sum_za, sum_rq, sum_aq, rows_sum(energy), 0.0, 0.0, 0.0))
+    gather_wait(2)
+    sums = jnp.sum(jnp.sum(gbuf2[...], axis=0), axis=1, keepdims=True)
+    rz, za, rq, aq, qq = (sums[k : k + 1] for k in range(5))
+
+    step1 = rz / za
+    rz_next = step1 * (step1 * aq - rq)
+    beta1 = 1.0 + rz_next / rz
+    norm2 = beta1 * beta1 * za - 2.0 * beta1 * step1 * aq + step1 * step1 * qq
+    step2 = rz_next / norm2
+    pressure_out[...] = (step1 + step2 * beta1) * search_ref[...] - (step2 * step1) * q
 
     for r, layers in enumerate((3, 1, 2, 1)):
         halo_drain(r, layers)
-    for g in range(5):
+    for g in range(3):
         gather_bytes(g, gsend_sem.at[g])
 
 
@@ -594,7 +603,9 @@
             pltpu.VMEM((4, 2, 24, 128), F32),
             pltpu.VMEM((4, 4, 8, 128), F32),
             pltpu.VMEM((4, 4, 8, 128), F32),
-            pltpu.VMEM((5, n, 2, 128), F32),
+            pltpu.VMEM((n, 2, 128), F32),
+            pltpu.VMEM((n, 1, 128), F32),
+            pltpu.VMEM((n, 8, 128), F32),
             pltpu.VMEM((ROWS, 128), F32),
             pltpu.VMEM((3 * ROWS, 128), F32),
             pltpu.VMEM((ROWS, 128), F32),
@@ -602,8 +613,8 @@
             *[pltpu.VMEM(t.shape, t.dtype) for t in consts],
             pltpu.SemaphoreType.DMA((4, 8)),
             pltpu.SemaphoreType.DMA((4, 8)),
-            pltpu.SemaphoreType.DMA((5,)),
-            pltpu.SemaphoreType.DMA((5,)),
+            pltpu.SemaphoreType.DMA((3,)),
+            pltpu.SemaphoreType.DMA((3,)),
             pltpu.SemaphoreType.DMA((10,)),
         ],
         compiler_params=pltpu.CompilerParams(

time: 39.2 us -> 35.7 us (0.911)
  Pallas kernels: 36.1 us -> 32.6 us
    pallas_call x1, Pallas kernels: 36.1 us -> 32.6 us  [body(): pl.pallas_call(functools.partial(kernel, ngx, ngy, gll_tables()[1]), out_...]
where the time goes in v2:
time: 35.7 us; the launch traced here: 35.5 us
  Pallas kernels  32.6 us (91%)
  local copies, waits for them, and re-layouts  2.26 us (6%)
  between operations  0.65 us (2%)
    pallas_call x1, Pallas kernels, body(): pl.pallas_call(functools.partial(kernel, ngx, ngy, gll_tables()[1]), out_...  32.6 us
    unnamed x4, local copies, waits for them, and re-layouts  2.26 us

profile of v2, /device:TPU:0, one launch (start us, length us, event | category | flops | bytes accessed | tf_op | source)
XLA Modules:
  0.0 35.5 jit_solution(5710686089180235643)
XLA Ops:
  0.6 32.6 %shard_map.113 = (f32[256,128]{1,0:T(8,128)}, f32[256,128]{1,0:T(8,128)}) custom-call(f32[256,128]{1,0:T(8,128)} %bitcast.6, f32[768,128]{1,0:T(8,128)} %bitcast.5, f32[256,128]{1,0:T(8,128)} %bitcast.7, s32[1,4,16]{2,1,0:T(4,128)} %solid_hbm.1, bf16[1280,256]{1,0:T(8,128)(2,1)} %constant.12.clone.refs_0_, bf16[1024,128]{1,0:T(8,128)(2,1)} %constant.13.clone.refs_1_, ...), custom_call_target="tpu_custom_call" | custom-call | tf_op jit(solution)/shard_map/pallas_call | solution.py:586
  33.2 0.0 copy-start
  33.3 1.6 %copy.14 = f32[8,32,128]{2,1,0:T(8,128)} copy(f32[8,32,128]{2,1,0:T(8,128)} %bitcast.9) | data formatting | bytes 262144
  34.9 0.0 copy-done
  34.9 0.7 %copy.15 = f32[8,32,128]{2,1,0:T(8,128)} copy(f32[8,32,128]{2,1,0:T(8,128)S(1)} %bitcast.8) | data formatting | bytes 262144
Async XLA Ops:
  33.2 1.6 %copy-start = (f32[256,128]{1,0:T(8,128)S(1)}, f32[256,128]{1,0:T(8,128)}, u32[]{:S(2)}) copy-start(f32[256,128]{1,0:T(8,128)} %get-tuple-element.5) | copy-start | bytes 393220

commit v3 on v2

--- a/solution.py
+++ b/solution.py
@@ -13,8 +13,10 @@
 EY = 4
 EX = 16
 ROWS = 256
-EXT = 384
+PLANE = 40
 SPEC = 400
+T_DY, T_DYT, T_DXT, T_DX, T_SX, T_BX = 0, 128, 256, 512, 768, 1152
+T_SY, T_BY, T_END = 1408, 1824, 2144
 
 TIME_STEP = 0.02
 HELM_COEF = 0.25
@@ -80,30 +82,18 @@
 def tables():
     weight, deriv = gll_tables()
     ids = np.arange(10) + 1.0
-    sine = np.sqrt(2.0 / 11.0) * np.sin(np.pi * np.outer(ids, ids) / 11.0)
+    sine = sine_table()
     eig = 2.0 - 2.0 * np.cos(np.pi * ids / 11.0)
-    dy = np.kron(np.eye(32), deriv)
+    dy = np.kron(np.eye(16), deriv)
     dx_t = np.kron(np.eye(EX), deriv.T)
     dx = np.kron(np.eye(EX), deriv)
 
-    def ext_row(z, y):
-        zlo, zhi, ylo, yhi = z < 0, z > 7, y < 0, y > 31
-        if zlo or zhi:
-            if ylo or yhi:
-                return 336 + 2 * int(zhi) + int(yhi)
-            return 256 + 32 * int(zhi) + y
-        if ylo or yhi:
-            return 320 + 8 * int(yhi) + z
-        return 32 * z + y
-
-    widen = np.zeros((SPEC, EXT))
-    for zi in range(10):
-        z = zi - 1
-        for e in range(EY):
-            for yi in range(10):
-                y = 8 * e - 2 if yi == 0 else (8 * e + 9 if yi == 9 else 8 * e + yi - 1)
-                widen[zi * 40 + e * 10 + yi, ext_row(z, y)] = 1.0
-    spec_zy = np.kron(sine, np.kron(np.eye(EY), sine)) @ widen
+    widen_y = np.zeros((PLANE, PLANE))
+    for e in range(EY):
+        for yi in range(10):
+            y = 8 * e - 2 if yi == 0 else (8 * e + 9 if yi == 9 else 8 * e + yi - 1)
+            widen_y[e * 10 + yi, 32 if y < 0 else (33 if y > 31 else y)] = 1.0
+    spec_y = np.kron(np.eye(5), np.kron(np.eye(EY), sine) @ widen_y)
     widen_x = np.zeros((160, 128))
     for e in range(EX):
         for xi in range(10):
@@ -112,7 +102,7 @@
                 widen_x[e * 10 + xi, x] = 1.0
     spec_x = np.zeros((128, 256))
     spec_x[:, :160] = (np.kron(np.eye(EX), sine) @ widen_x).T
-    back_zy = np.kron(sine[1:9], np.kron(np.eye(EY), sine[1:9]))
+    back_y = np.kron(np.eye(5), np.kron(np.eye(EY), sine[1:9]))
     back_x = np.zeros((256, 128))
     back_x[:160] = np.kron(np.eye(EX), sine[1:9]).T
     lam_zy = (eig[:, None] + np.tile(eig, EY)[None, :]).reshape(SPEC)
@@ -126,17 +116,42 @@
     spread = np.zeros((16, 128))
     spread[:EX] = np.kron(np.eye(EX), np.ones((1, 8)))
 
-    def stack(*parts):
-        return np.concatenate([half for part in parts for half in halves(part)], axis=0)
+    def beside(table):
+        high, low = halves(table)
+        return np.concatenate([high, low], axis=1)
+
+    def both(table):
+        high, low = halves(table)
+        zero = np.zeros_like(low)
+        return np.concatenate(
+            [np.concatenate([high, low], axis=1), np.concatenate([high, zero], axis=1)], axis=0
+        )
+
+    def under(table):
+        high, low = halves(table)
+        return np.concatenate([high, high, low], axis=0)
+
+    def padded(table, rows, cols):
+        out = np.zeros((rows, cols))
+        out[: table.shape[0], : table.shape[1]] = table
+        return out
 
     return (
-        stack(dy, dy.T, spec_x),
-        stack(dx_t, dx, back_x),
+        np.concatenate(
+            [
+                beside(dy), beside(dy.T), both(dx_t), both(dx), under(spec_x), beside(back_x),
+                *halves(padded(spec_y, 208, 256)), *halves(padded(back_y, 160, 256)),
+            ],
+            axis=0,
+        ),
         np.concatenate([mass, spread], axis=0).astype(np.float32),
-        stack(spec_zy),
         inv_den.astype(np.float32),
-        stack(back_zy),
-    )
+    )
+
+
+def sine_table():
+    ids = np.arange(10) + 1.0
+    return np.sqrt(2.0 / 11.0) * np.sin(np.pi * np.outer(ids, ids) / 11.0)
 
 
 def split(v):
@@ -149,16 +164,35 @@
     return jnp.dot(a, b, preferred_element_type=F32)
 
 
-def left(ref, base, rows, v):
+def along_y(v, ref, base):
+    vh, vl = split(jnp.concatenate([v[:128], v[128:]], axis=1))
+    table = ref[base : base + 128, :]
+    out = dot(table, jnp.concatenate([vh, vh], axis=0)) + dot(table[:, :128], vl)
+    return jnp.concatenate([out[:, :128], out[:, 128:]], axis=0)
+
+
+def along_x(v, ref, base):
     vh, vl = split(v)
-    both = dot(ref[base : base + rows, :], jnp.concatenate([vh, vl], axis=1))
-    return both[:, :128] + both[:, 128:] + dot(ref[base + rows : base + 2 * rows, :], vh)
-
-
-def right(v, ref, base, rows):
-    vh, vl = split(v)
-    high = ref[base : base + rows, :]
-    return dot(vh, high) + dot(vl, high) + dot(vh, ref[base + rows : base + 2 * rows, :])
+    out = dot(jnp.concatenate([vh, vl], axis=1), ref[base : base + 256, :])
+    return out[:, :128] + out[:, 128:]
+
+
+def planes_y(v, ref, base, rows, pad):
+    vh, vl = split(jnp.concatenate([v[:200], v[200:]], axis=1))
+    high = ref[base : base + pad, :200]
+    low = ref[base + pad : base + 2 * pad, :200]
+    out = dot(high, vh) + dot(high, vl) + dot(low, vh)
+    return jnp.concatenate([out[:rows, :128], out[:rows, 128:]], axis=0)
+
+
+def sine_z(planes, sine, keep):
+    even = [planes[k] + planes[9 - k] for k in range(5)]
+    odd = [planes[k] - planes[9 - k] for k in range(5)]
+    out = []
+    for j in keep:
+        terms = [float(sine[j, k]) * (odd if j % 2 else even)[k] for k in range(5)]
+        out.append(functools.reduce(lambda a, b: a + b, terms))
+    return out
 
 
 def along_z(v, table):
@@ -189,16 +223,16 @@
 
 
 def kernel(
-    ngx, ngy, deriv,
+    ngx, ngy, deriv, sine,
     level_hbm, vel_hbm, source_hbm, solid_hbm, *refs
 ):
-    tables_hbm, refs = refs[:6], refs[6:]
+    tables_hbm, refs = refs[:3], refs[3:]
     level_out, pressure_out = refs[:2]
     (
-        flux_ref, invm_ref, part_ref, lev_ref, app_ref, res_ref, search_ref, a_ref,
+        flux_ref, invm_ref, part_ref, lev_ref, app_ref, res_ref, search_ref, ext_ref, a_ref,
         zs, zr, ys, yr, cs, cr, gbuf0, gbuf1, gbuf2,
         level_ref, vel_ref, source_ref, solid_ref,
-        t256, t128, mass_ref, spec_ref, den_ref, back_ref,
+        table, mass_ref, den_ref,
         send_sem, recv_sem, gsend_sem, grecv_sem, load_sem,
     ) = refs[2:]
     loads = [
@@ -207,11 +241,11 @@
             zip(
                 (level_hbm, vel_hbm, source_hbm, solid_hbm) + tables_hbm,
                 (level_ref, vel_ref, source_ref, solid_ref)
-                + (t256, t128, mass_ref, spec_ref, den_ref, back_ref),
+                + (table, mass_ref, den_ref),
             )
         )
     ]
-    for i in (4, 5, 0, 1, 6, 2, 3, 7, 8, 9):
+    for i in (4, 0, 1, 5, 2, 3, 6):
         loads[i].start()
     gbufs = (gbuf0, gbuf1, gbuf2)
     n = ngx * ngy
@@ -226,6 +260,7 @@
     zr[...] = jnp.zeros_like(zr)
     yr[...] = jnp.zeros_like(yr)
     cr[...] = jnp.zeros_like(cr)
+    ext_ref[...] = jnp.zeros_like(ext_ref)
 
     barrier = pltpu.get_barrier_semaphore()
 
@@ -331,19 +366,19 @@
         for c, row in enumerate((0, 31, 224, 255)):
             ref[row : row + 1] = ref[row : row + 1] + cr[r, c, crow : crow + 1]
 
-    def outer_halo(r, ref):
+    def outer_halo(r):
         for s in range(2):
-            base = 256 + 32 * s
-            ref[base : base + 32] = zr[r, s, 32:64]
-            ref[base : base + 1] = ref[base : base + 1] + cr[r, 2 * s, 2:3]
-            ref[base + 31 : base + 32] = ref[base + 31 : base + 32] + cr[r, 2 * s + 1, 2:3]
-            base = 320 + 8 * s
-            ref[base : base + 8] = yr[r, s, 8:16]
-            ref[base : base + 1] = ref[base : base + 1] + cr[r, s, 1:2]
-            ref[base + 7 : base + 8] = ref[base + 7 : base + 8] + cr[r, 2 + s, 1:2]
-        ref[336:384] = jnp.zeros((48, 128), F32)
+            base = 9 * PLANE * s
+            ext_ref[base : base + 32] = zr[r, s, 32:64]
+            ext_ref[base : base + 1] = ext_ref[base : base + 1] + cr[r, 2 * s, 2:3]
+            at = base + 31
+            ext_ref[at : at + 1] = ext_ref[at : at + 1] + cr[r, 2 * s + 1, 2:3]
+            ext_ref[pl.ds(PLANE + 32 + s, 8, stride=PLANE), :] = yr[r, s, 8:16]
+            for at, c in ((PLANE + 32 + s, s), (8 * PLANE + 32 + s, 2 + s)):
+                ext_ref[at : at + 1] = ext_ref[at : at + 1] + cr[r, c, 1:2]
         for c in range(4):
-            ref[336 + c : 337 + c] = cr[r, c, 3:4]
+            at = 9 * PLANE * (c // 2) + 32 + c % 2
+            ext_ref[at : at + 1] = cr[r, c, 3:4]
 
     def gather_copy(g, dst):
         ref = gbufs[g].at[me]
@@ -402,27 +437,27 @@
         v = v + x_first * pltpu.roll(v, 1, 1) + x_last * pltpu.roll(v, 127, 1)
         return v + y_first * pltpu.roll(v, 1, 0) + y_last * pltpu.roll(v, ROWS - 1, 0)
 
-    for i in (4, 5, 0, 1, 6):
+    for i in (4, 0, 1, 5):
         loads[i].wait()
     mass = mass_ref[0:ROWS]
     level = level_ref[...]
     advect = (
         vel_ref[0:ROWS] * along_z(level, deriv)
-        + vel_ref[ROWS : 2 * ROWS] * left(t256, 0, ROWS, level)
-        + vel_ref[2 * ROWS : 3 * ROWS] * right(level, t128, 0, 128)
+        + vel_ref[ROWS : 2 * ROWS] * along_y(level, table, T_DY)
+        + vel_ref[2 * ROWS : 3 * ROWS] * along_x(level, table, T_DXT)
     )
     lev_ref[...] = fold_in(mass * (level - (2.0 * TIME_STEP) * advect))
     diverge = (
         along_z(vel_ref[0:ROWS], deriv)
-        + left(t256, 0, ROWS, vel_ref[ROWS : 2 * ROWS])
-        + right(vel_ref[2 * ROWS : 3 * ROWS], t128, 0, 128)
+        + along_y(vel_ref[ROWS : 2 * ROWS], table, T_DY)
+        + along_x(vel_ref[2 * ROWS : 3 * ROWS], table, T_DXT)
     )
     loads[2].wait()
     part_ref[...] = fold_in(mass * (source_ref[...] - (2.0 * TIME_STEP) * diverge))
 
     pl.semaphore_wait(barrier, n - 1)
     halo_send(0, 3, lev_ref)
-    res_ref[0:ROWS] = part_ref[...]
+    res_ref[...] = part_ref[...]
     loads[3].wait()
     solid = dot(solid_ref[0].astype(F32), mass_ref[ROWS : ROWS + EX])
     solid = jnp.concatenate(
@@ -432,25 +467,36 @@
     halo_wait(0, 3)
     add_rim(0, res_ref, 0, 0, 0)
     add_rim(0, lev_ref, 64, 16, 4)
-    outer_halo(0, res_ref)
+    outer_halo(0)
     level_new = lev_ref[...] * inv_m / mass
     level_out[...] = level_new
     coef = (GAS_RATIO - (GAS_RATIO - 1.0) * jax.nn.sigmoid(level_new / LEVEL_WIDTH)) * (
         1.0 - (1.0 - SOLID_FACTOR) * solid
     )
     flux_ref[...] = 4.0 * coef * mass
-    gather_send(0, (total(coef) / (ROWS * 128.0), total(res_ref[0:ROWS] * inv_m)))
-
-    def local_solve(ref):
-        spectral = right(left(spec_ref, 0, SPEC, ref[...]), t256, 4 * ROWS, 128)
-        spectral = spectral * den_ref[...]
-        return left(back_ref, 0, ROWS, right(spectral, t128, 512, 256))
+    gather_send(0, (total(coef) / (ROWS * 128.0), total(res_ref[...] * inv_m)))
+
+    def local_solve(v):
+        for z in range(8):
+            ext_ref[PLANE * (z + 1) : PLANE * (z + 1) + 32] = v[32 * z : 32 * z + 32]
+        planes = [ext_ref[PLANE * z : PLANE * z + PLANE] for z in range(10)]
+        wide = jnp.concatenate(sine_z(planes, sine, range(10)), axis=0)
+        wide = planes_y(wide, table, T_SY, 200, 208)
+        wh, wl = split(wide)
+        spectral = dot(jnp.concatenate([wh, wl], axis=1), table[T_SX : T_SX + 256, :])
+        spectral = spectral + dot(wh, table[T_SX + 256 : T_SX + 384, :])
+        sh, sl = split(spectral * den_ref[...])
+        back = dot(sh, table[T_BX : T_BX + 256, :])
+        back = back[:, :128] + back[:, 128:] + dot(sl, table[T_BX : T_BX + 256, :128])
+        back = planes_y(back, table, T_BY, 160, 160)
+        planes = [back[32 * z : 32 * z + 32] for z in range(10)]
+        return jnp.concatenate(sine_z(planes, sine, range(1, 9)), axis=0)
 
     def helm(v):
         flux = flux_ref[...]
         out = along_z(flux * along_z(v, deriv), deriv.T)
-        out = out + left(t256, 2 * ROWS, ROWS, flux * left(t256, 0, ROWS, v))
-        out = out + right(flux * right(v, t128, 0, 128), t128, 256, 128)
+        out = out + along_y(flux * along_y(v, table, T_DY), table, T_DYT)
+        out = out + along_x(flux * along_x(v, table, T_DXT), table, T_DX)
         return out + HELM_COEF * mass_ref[0:ROWS] * v
 
     npad = a_ref.shape[1]
@@ -475,22 +521,31 @@
         link = 2.0 * k_col * k_row / (k_col + k_row) * rate
         diagonal = HELM_COEF * EZ * EY * EX + jnp.sum(link, axis=1, keepdims=True)
         a = jnp.where(diag, diagonal, -link)
-        if n <= 64 and n % 2 == 0:
-            for k in range(0, n, 2):
-                c1 = jnp.broadcast_to(a[:, k : k + 1], (n, npad))
-                c2 = jnp.broadcast_to(a[:, k + 1 : k + 2], (n, npad))
-                p11, p12, p22 = c1[k : k + 1], c2[k : k + 1], c2[k + 1 : k + 2]
-                scale = 1.0 / (p11 * p22 - p12 * p12)
-                at1, at2 = lane_n == k, lane_n == k + 1
-                on1, on2 = sub_n == k, sub_n == k + 1
-                r1 = jnp.where(at1[:1], -1.0, jnp.where(at2[:1], 0.0, a[k : k + 1]))
-                r2 = jnp.where(at2[:1], -1.0, jnp.where(at1[:1], 0.0, a[k + 1 : k + 2]))
-                q1 = (p22 * r1 - p12 * r2) * scale
-                q2 = (p11 * r2 - p12 * r1) * scale
-                c1 = jnp.where(on1, -1.0, jnp.where(on2, 0.0, c1))
-                c2 = jnp.where(on2, -1.0, jnp.where(on1, 0.0, c2))
-                cross = jnp.logical_or(jnp.logical_or(at1, at2), jnp.logical_or(on1, on2))
-                a = jnp.where(cross, 0.0, a) - c1 * q1 - c2 * q2
+        if ngx == 2 and n <= 64:
+            left_over = list(range(ngy))
+            while left_over:
+                now = left_over[1::2] or left_over
+                left_over = left_over[0::2] if len(left_over) > 1 else []
+                cross = jnp.zeros((n, npad), jnp.bool_)
+                change = None
+                for j in now:
+                    k, m = j, ngy + j
+                    c1 = jnp.broadcast_to(a[:, k : k + 1], (n, npad))
+                    c2 = jnp.broadcast_to(a[:, m : m + 1], (n, npad))
+                    p11, p12, p22 = c1[k : k + 1], c2[k : k + 1], c2[m : m + 1]
+                    scale = 1.0 / (p11 * p22 - p12 * p12)
+                    at1, at2 = lane_n == k, lane_n == m
+                    on1, on2 = sub_n == k, sub_n == m
+                    r1 = jnp.where(at1[:1], -1.0, jnp.where(at2[:1], 0.0, a[k : k + 1]))
+                    r2 = jnp.where(at2[:1], -1.0, jnp.where(at1[:1], 0.0, a[m : m + 1]))
+                    q1 = (p22 * r1 - p12 * r2) * scale
+                    q2 = (p11 * r2 - p12 * r1) * scale
+                    c1 = jnp.where(on1, -1.0, jnp.where(on2, 0.0, c1))
+                    c2 = jnp.where(on2, -1.0, jnp.where(on1, 0.0, c2))
+                    cross = cross | at1 | at2 | on1 | on2
+                    term = c1 * q1 + c2 * q2
+                    change = term if change is None else change + term
+                a = jnp.where(cross, 0.0, a) - change
             a_ref[...] = a
         else:
             a_ref[...] = a
@@ -520,9 +575,8 @@
     def rows_sum(v):
         return jnp.sum(v, axis=0, keepdims=True)
 
-    for i in (7, 8, 9):
-        loads[i].wait()
-    part_ref[...] = fold_in(local_solve(res_ref) * inv_m)
+    loads[6].wait()
+    part_ref[...] = fold_in(local_solve(res_ref[...]) * inv_m)
     halo_send(1, 1)
     gather_wait(0)
     invert(gathered(0, 0))
@@ -536,15 +590,15 @@
     applied = helm(z1)
     part_ref[...] = fold_in(applied)
     halo_send(2, 2)
-    sum_rz = rows_sum(res_ref[0:ROWS] * z1 * inv_m)
+    sum_rz = rows_sum(res_ref[...] * z1 * inv_m)
     sum_za = rows_sum(z1 * applied)
-    app_ref[0:ROWS] = part_ref[...]
+    app_ref[...] = part_ref[...]
     halo_wait(2, 2)
     add_rim(2, app_ref, 0, 0, 0)
-    outer_halo(2, app_ref)
-    gather_send(1, (total(app_ref[0:ROWS] * invm_ref[...]),))
-
-    part_ref[...] = fold_in(local_solve(app_ref) * invm_ref[...])
+    outer_halo(2)
+    gather_send(1, (total(app_ref[...] * invm_ref[...]),))
+
+    part_ref[...] = fold_in(local_solve(app_ref[...]) * invm_ref[...])
     halo_send(3, 1)
     gather_wait(1)
     field = coarse_field(coarse(gathered(1, 0)))
@@ -553,11 +607,11 @@
     q = part_ref[...] + field
 
     q_m = q * invm_ref[...]
-    gz, gy, gx = along_z(q, deriv), left(t256, 0, ROWS, q), right(q, t128, 0, 128)
+    gz, gy, gx = along_z(q, deriv), along_y(q, table, T_DY), along_x(q, table, T_DXT)
     energy = flux_ref[...] * (gz * gz + gy * gy + gx * gx)
     energy = energy + HELM_COEF * mass_ref[0:ROWS] * (q * q)
-    sum_rq = rows_sum(res_ref[0:ROWS] * q_m)
-    sum_aq = rows_sum(app_ref[0:ROWS] * q_m)
+    sum_rq = rows_sum(res_ref[...] * q_m)
+    sum_aq = rows_sum(app_ref[...] * q_m)
     gather_send(2, (sum_rz, sum_za, sum_rq, sum_aq, rows_sum(energy), 0.0, 0.0, 0.0))
     gather_wait(2)
     sums = jnp.sum(jnp.sum(gbuf2[...], axis=0), axis=1, keepdims=True)
@@ -584,7 +638,7 @@
     vmem = pl.BlockSpec(memory_space=pltpu.VMEM)
     shape = level_set.shape
     level_new, pressure = pl.pallas_call(
-        functools.partial(kernel, ngx, ngy, gll_tables()[1]),
+        functools.partial(kernel, ngx, ngy, gll_tables()[1], sine_table()),
         out_shape=[jax.ShapeDtypeStruct((ROWS, 128), F32)] * 2,
         in_specs=[hbm] * (4 + len(consts)),
         out_specs=[vmem] * 2,
@@ -593,9 +647,10 @@
             pltpu.VMEM((ROWS, 128), F32),
             pltpu.VMEM((ROWS, 128), F32),
             pltpu.VMEM((ROWS, 128), F32),
-            pltpu.VMEM((EXT, 128), F32),
-            pltpu.VMEM((EXT, 128), F32),
-            pltpu.VMEM((ROWS, 128), F32),
+            pltpu.VMEM((ROWS, 128), F32),
+            pltpu.VMEM((ROWS, 128), F32),
+            pltpu.VMEM((ROWS, 128), F32),
+            pltpu.VMEM((SPEC, 128), F32),
             pltpu.VMEM((n, npad), F32),
             pltpu.VMEM((4, 2, 96, 128), F32),
             pltpu.VMEM((4, 2, 96, 128), F32),
@@ -615,7 +670,7 @@
             pltpu.SemaphoreType.DMA((4, 8)),
             pltpu.SemaphoreType.DMA((3,)),
             pltpu.SemaphoreType.DMA((3,)),
-            pltpu.SemaphoreType.DMA((10,)),
+            pltpu.SemaphoreType.DMA((7,)),
         ],
         compiler_params=pltpu.CompilerParams(
             collective_id=0, has_side_effects=True, vmem_limit_bytes=63 * 1024 * 1024

time: 35.7 us -> 35 us (0.980)
  Pallas kernels: 32.6 us -> 31.1 us
  local copies, waits for them, and re-layouts: 2.26 us -> 3.14 us
    pallas_call x1, Pallas kernels: 32.6 us -> 31.1 us  [body(): pl.pallas_call(functools.partial(kernel, ngx, ngy, gll_tables()[1], sine_...]
    unnamed x4 -> x2, local copies, waits for them, and re-layouts: 2.26 us -> 3.14 us
where the time goes in v3:
time: 35 us; the launch traced here: 34.9 us
  Pallas kernels  31.1 us (89%)
  local copies, waits for them, and re-layouts  3.14 us (9%)
  between operations  0.64 us (2%)
    pallas_call x1, Pallas kernels, body(): pl.pallas_call(functools.partial(kernel, ngx, ngy, gll_tables()[1], sine_...  31.1 us
    unnamed x2, local copies, waits for them, and re-layouts  3.14 us

profile of v3, /device:TPU:0, one launch (start us, length us, event | category | flops | bytes accessed | tf_op | source)
XLA Modules:
  0.0 34.9 jit_solution(15458259072740319445)
XLA Ops:
  0.6 31.1 %shard_map.86 = (f32[256,128]{1,0:T(8,128)}, f32[256,128]{1,0:T(8,128)}) custom-call(f32[256,128]{1,0:T(8,128)} %bitcast.8, f32[768,128]{1,0:T(8,128)} %bitcast.5, f32[256,128]{1,0:T(8,128)} %bitcast.9, s32[1,4,16]{2,1,0:T(4,128)} %solid_hbm.1, bf16[2144,256]{1,0:T(8,128)(2,1)} %constant.6.clone.refs_0_, f32[272,128]{1,0:T(8,128)} %constant.7.clone.refs_1_, ...), custom_call_target="tpu_custom_call" | custom-call | tf_op jit(solution)/shard_map/pallas_call | solution.py:640
  31.7 1.6 %copy.11 = f32[8,32,128]{2,1,0:T(8,128)} copy(f32[8,32,128]{2,1,0:T(8,128)} %bitcast.7) | data formatting | bytes 262144
  33.3 1.6 %copy.12 = f32[8,32,128]{2,1,0:T(8,128)} copy(f32[8,32,128]{2,1,0:T(8,128)} %bitcast.6) | data formatting | bytes 262144

commit v4 on v3

--- a/solution.py
+++ b/solution.py
@@ -673,7 +673,7 @@
             pltpu.SemaphoreType.DMA((7,)),
         ],
         compiler_params=pltpu.CompilerParams(
-            collective_id=0, has_side_effects=True, vmem_limit_bytes=63 * 1024 * 1024
+            collective_id=0, has_side_effects=True, vmem_limit_bytes=54848 * 1024
         ),
     )(
         level_set.reshape(ROWS, 128),

time: 35 us -> 33.2 us (0.949)
  local copies, waits for them, and re-layouts: 3.14 us -> 1.99 us
  Pallas kernels: 31.1 us -> 30.4 us
    unnamed x2 -> x4, local copies, waits for them, and re-layouts: 3.14 us -> 1.99 us
    pallas_call x1, Pallas kernels: 31.1 us -> 30.4 us  [body(): pl.pallas_call(functools.partial(kernel, ngx, ngy, gll_tables()[1], sine_...]
where the time goes in v4:
time: 33.2 us; the launch traced here: 33 us
  Pallas kernels  30.4 us (92%)
  local copies, waits for them, and re-layouts  1.99 us (6%)
  between operations  0.65 us (2%)
    pallas_call x1, Pallas kernels, body(): pl.pallas_call(functools.partial(kernel, ngx, ngy, gll_tables()[1], sine_...  30.4 us
    unnamed x4, local copies, waits for them, and re-layouts  1.99 us

profile of v4, /device:TPU:0, one launch (start us, length us, event | category | flops | bytes accessed | tf_op | source)
XLA Modules:
  0.0 33.0 jit_solution(4179940853004936421)
XLA Ops:
  0.6 0.0 copy-start
  0.6 0.7 %copy-done = s32[1,4,16]{2,1,0:T(4,128)S(1)} copy-done((s32[1,4,16]{2,1,0:T(4,128)S(1)}, s32[1,4,16]{2,1,0:T(4,128)}, u32[]{:S(2)}) %copy-start) | copy-done | bytes 280
  1.3 30.4 %shard_map.86 = (f32[256,128]{1,0:T(8,128)S(1)}, f32[256,128]{1,0:T(8,128)S(1)}) custom-call(f32[256,128]{1,0:T(8,128)} %bitcast.8, f32[768,128]{1,0:T(8,128)} %bitcast.7, f32[256,128]{1,0:T(8,128)} %bitcast.9, s32[1,4,16]{2,1,0:T(4,128)S(1)} %copy-done, bf16[2144,256]{1,0:T(8,128)(2,1)} %constant.6.clone.refs_0_, f32[272,128]{1,0:T(8,128)} %constant.7.clone.refs_1_, ...), custom_call_target="tpu_custom_call" | custom-call | tf_op jit(solution)/shard_map/pallas_call | solution.py:640
  31.7 0.7 %copy.11 = f32[8,32,128]{2,1,0:T(8,128)} copy(f32[8,32,128]{2,1,0:T(8,128)S(1)} %bitcast.6) | data formatting | bytes 262144
  32.3 0.7 %copy.12 = f32[8,32,128]{2,1,0:T(8,128)} copy(f32[8,32,128]{2,1,0:T(8,128)S(1)} %bitcast.5) | data formatting | bytes 262144
Async XLA Ops:
  0.6 0.7 %copy-start = (s32[1,4,16]{2,1,0:T(4,128)S(1)}, s32[1,4,16]{2,1,0:T(4,128)}, u32[]{:S(2)}) copy-start(s32[1,4,16]{2,1,0:T(4,128)} %solid_hbm.1) | copy-start | bytes 772

commit v5 on v4

--- a/solution.py
+++ b/solution.py
@@ -235,17 +235,21 @@
         table, mass_ref, den_ref,
         send_sem, recv_sem, gsend_sem, grecv_sem, load_sem,
     ) = refs[2:]
+    first, later = pl.ds(0, T_SX), pl.ds(T_SX, T_END - T_SX)
+    pairs = (
+        (level_hbm, level_ref),
+        (vel_hbm, vel_ref),
+        (source_hbm, source_ref),
+        (solid_hbm, solid_ref),
+        (tables_hbm[0].at[first], table.at[first]),
+        (tables_hbm[1], mass_ref),
+        (tables_hbm[2], den_ref),
+        (tables_hbm[0].at[later], table.at[later]),
+    )
     loads = [
-        pltpu.make_async_copy(src, dst, load_sem.at[i])
-        for i, (src, dst) in enumerate(
-            zip(
-                (level_hbm, vel_hbm, source_hbm, solid_hbm) + tables_hbm,
-                (level_ref, vel_ref, source_ref, solid_ref)
-                + (table, mass_ref, den_ref),
-            )
-        )
+        pltpu.make_async_copy(src, dst, load_sem.at[i]) for i, (src, dst) in enumerate(pairs)
     ]
-    for i in (4, 0, 1, 5, 2, 3, 6):
+    for i in (0, 4, 1, 5, 2, 3, 7, 6):
         loads[i].start()
     gbufs = (gbuf0, gbuf1, gbuf2)
     n = ngx * ngy
@@ -576,6 +580,7 @@
         return jnp.sum(v, axis=0, keepdims=True)
 
     loads[6].wait()
+    loads[7].wait()
     part_ref[...] = fold_in(local_solve(res_ref[...]) * inv_m)
     halo_send(1, 1)
     gather_wait(0)
@@ -613,6 +618,10 @@
     sum_rq = rows_sum(res_ref[...] * q_m)
     sum_aq = rows_sum(app_ref[...] * q_m)
     gather_send(2, (sum_rz, sum_za, sum_rq, sum_aq, rows_sum(energy), 0.0, 0.0, 0.0))
+    for r, layers in enumerate((3, 1, 2, 1)):
+        halo_drain(r, layers)
+    for g in range(2):
+        gather_bytes(g, gsend_sem.at[g])
     gather_wait(2)
     sums = jnp.sum(jnp.sum(gbuf2[...], axis=0), axis=1, keepdims=True)
     rz, za, rq, aq, qq = (sums[k : k + 1] for k in range(5))
@@ -624,10 +633,7 @@
     step2 = rz_next / norm2
     pressure_out[...] = (step1 + step2 * beta1) * search_ref[...] - (step2 * step1) * q
 
-    for r, layers in enumerate((3, 1, 2, 1)):
-        halo_drain(r, layers)
-    for g in range(3):
-        gather_bytes(g, gsend_sem.at[g])
+    gather_bytes(2, gsend_sem.at[2])
 
 
 def body(ngx, ngy, level_set, velocity, source, wick_solid):
@@ -670,7 +676,7 @@
             pltpu.SemaphoreType.DMA((4, 8)),
             pltpu.SemaphoreType.DMA((3,)),
             pltpu.SemaphoreType.DMA((3,)),
-            pltpu.SemaphoreType.DMA((7,)),
+            pltpu.SemaphoreType.DMA((8,)),
         ],
         compiler_params=pltpu.CompilerParams(
             collective_id=0, has_side_effects=True, vmem_limit_bytes=54848 * 1024

time: 33.2 us -> 33.1 us (level)
  no operation moved by 1% of the time
where the time goes in v5:
time: 33.1 us; the launch traced here: 33 us
  Pallas kernels  30.3 us (92%)
  local copies, waits for them, and re-layouts  1.99 us (6%)
  between operations  0.65 us (2%)
    pallas_call x1, Pallas kernels, body(): pl.pallas_call(functools.partial(kernel, ngx, ngy, gll_tables()[1], sine_...  30.3 us
    unnamed x4, local copies, waits for them, and re-layouts  1.99 us

profile of v5, /device:TPU:0, one launch (start us, length us, event | category | flops | bytes accessed | tf_op | source)
XLA Modules:
  0.0 33.0 jit_solution(9359961740706705314)
XLA Ops:
  0.6 0.0 copy-start
  0.6 0.7 %copy-done = s32[1,4,16]{2,1,0:T(4,128)S(1)} copy-done((s32[1,4,16]{2,1,0:T(4,128)S(1)}, s32[1,4,16]{2,1,0:T(4,128)}, u32[]{:S(2)}) %copy-start) | copy-done | bytes 280
  1.3 30.3 %shard_map.86 = (f32[256,128]{1,0:T(8,128)S(1)}, f32[256,128]{1,0:T(8,128)S(1)}) custom-call(f32[256,128]{1,0:T(8,128)} %bitcast.8, f32[768,128]{1,0:T(8,128)} %bitcast.7, f32[256,128]{1,0:T(8,128)} %bitcast.9, s32[1,4,16]{2,1,0:T(4,128)S(1)} %copy-done, bf16[2144,256]{1,0:T(8,128)(2,1)} %constant.6.clone.refs_0_, f32[272,128]{1,0:T(8,128)} %constant.7.clone.refs_1_, ...), custom_call_target="tpu_custom_call" | custom-call | tf_op jit(solution)/shard_map/pallas_call | solution.py:646
  31.7 0.7 %copy.11 = f32[8,32,128]{2,1,0:T(8,128)} copy(f32[8,32,128]{2,1,0:T(8,128)S(1)} %bitcast.6) | data formatting | bytes 262144
  32.3 0.7 %copy.12 = f32[8,32,128]{2,1,0:T(8,128)} copy(f32[8,32,128]{2,1,0:T(8,128)S(1)} %bitcast.5) | data formatting | bytes 262144
Async XLA Ops:
  0.6 0.7 %copy-start = (s32[1,4,16]{2,1,0:T(4,128)S(1)}, s32[1,4,16]{2,1,0:T(4,128)}, u32[]{:S(2)}) copy-start(s32[1,4,16]{2,1,0:T(4,128)} %solid_hbm.1) | copy-start | bytes 772

commit v6 on v5

--- a/solution.py
+++ b/solution.py
@@ -576,6 +576,26 @@
 
         return own_z * along_y(0) + half_zlo * along_y(-1) + half_zhi * along_y(1)
 
+    offsets = [(dz, dy) for dz in (0, -1, 1) for dy in (0, -1, 1)]
+
+    def shares(v):
+        row = jnp.zeros((1, 128), F32)
+        for d, (dz, dy) in enumerate(offsets):
+            part = v * (own_z, half_zhi, half_zlo)[dz] * (own_y, half_yhi, half_ylo)[dy]
+            row = row + jnp.where(lane[:1] == d, total(part), 0.0)
+        return row
+
+    def share_totals():
+        got = gbufs[1][:, 0, :]
+        out = jnp.zeros((n, 128), F32)
+        for d, (dz, dy) in enumerate(offsets):
+            value = jnp.broadcast_to(got[:, d : d + 1], (n, 128))
+            shift = (dz * ngy + dy) % n
+            if shift:
+                value = jnp.concatenate([value[n - shift :], value[: n - shift]], axis=0)
+            out = out + value
+        return out if npad == 128 else jnp.concatenate([out] * (npad // 128), axis=1)
+
     def rows_sum(v):
         return jnp.sum(v, axis=0, keepdims=True)
 
@@ -595,18 +615,18 @@
     applied = helm(z1)
     part_ref[...] = fold_in(applied)
     halo_send(2, 2)
+    gather_send(1, (shares(applied),))
     sum_rz = rows_sum(res_ref[...] * z1 * inv_m)
     sum_za = rows_sum(z1 * applied)
     app_ref[...] = part_ref[...]
     halo_wait(2, 2)
     add_rim(2, app_ref, 0, 0, 0)
     outer_halo(2)
-    gather_send(1, (total(app_ref[...] * invm_ref[...]),))
 
     part_ref[...] = fold_in(local_solve(app_ref[...]) * invm_ref[...])
     halo_send(3, 1)
     gather_wait(1)
-    field = coarse_field(coarse(gathered(1, 0)))
+    field = coarse_field(coarse(share_totals()))
     halo_wait(3, 1)
     add_rim(3, part_ref, 0, 0, 0)
     q = part_ref[...] + field

time: 33.1 us -> 33.1 us (level)
  no operation moved by 1% of the time
where the time goes in v6:
time: 33.1 us; the launch traced here: 33 us
  Pallas kernels  30.3 us (92%)
  local copies, waits for them, and re-layouts  1.99 us (6%)
  between operations  0.65 us (2%)
    pallas_call x1, Pallas kernels, body(): pl.pallas_call(functools.partial(kernel, ngx, ngy, gll_tables()[1], sine_...  30.3 us
    unnamed x4, local copies, waits for them, and re-layouts  1.99 us

profile of v6, /device:TPU:0, one launch (start us, length us, event | category | flops | bytes accessed | tf_op | source)
XLA Modules:
  0.0 33.0 jit_solution(9190901048487989610)
XLA Ops:
  0.6 0.0 copy-start
  0.6 0.7 %copy-done = s32[1,4,16]{2,1,0:T(4,128)S(1)} copy-done((s32[1,4,16]{2,1,0:T(4,128)S(1)}, s32[1,4,16]{2,1,0:T(4,128)}, u32[]{:S(2)}) %copy-start) | copy-done | bytes 280
  1.3 30.3 %shard_map.86 = (f32[256,128]{1,0:T(8,128)S(1)}, f32[256,128]{1,0:T(8,128)S(1)}) custom-call(f32[256,128]{1,0:T(8,128)} %bitcast.8, f32[768,128]{1,0:T(8,128)} %bitcast.7, f32[256,128]{1,0:T(8,128)} %bitcast.9, s32[1,4,16]{2,1,0:T(4,128)S(1)} %copy-done, bf16[2144,256]{1,0:T(8,128)(2,1)} %constant.6.clone.refs_0_, f32[272,128]{1,0:T(8,128)} %constant.7.clone.refs_1_, ...), custom_call_target="tpu_custom_call" | custom-call | tf_op jit(solution)/shard_map/pallas_call | solution.py:666
  31.6 0.7 %copy.11 = f32[8,32,128]{2,1,0:T(8,128)} copy(f32[8,32,128]{2,1,0:T(8,128)S(1)} %bitcast.6) | data formatting | bytes 262144
  32.3 0.7 %copy.12 = f32[8,32,128]{2,1,0:T(8,128)} copy(f32[8,32,128]{2,1,0:T(8,128)S(1)} %bitcast.5) | data formatting | bytes 262144
Async XLA Ops:
  0.6 0.7 %copy-start = (s32[1,4,16]{2,1,0:T(4,128)S(1)}, s32[1,4,16]{2,1,0:T(4,128)}, u32[]{:S(2)}) copy-start(s32[1,4,16]{2,1,0:T(4,128)} %solid_hbm.1) | copy-start | bytes 772
